TPU v7x, 32 devices: a whole 2x2x4 slice. The times are simulated.
32 devices in a mesh: batch: 8 (over z, x), chan: 4 (over y, core).
Axes of the slice: x: 2, y: 2, z: 4, core: 2. Of those that a mesh axis runs over, the one named last changes fastest.
Arguments:
- block_input: bfloat16 [128, 14, 14, 1024], P('batch', None, None, 'chan'), may hold values from -6 to 6
- first_reduce: float32 [1024, 512], P('batch', 'chan'), may hold values from -0.1875 to 0.1875
- first_spatial: float32 [3, 3, 512, 512], P(None, None, 'batch', 'chan'), may hold values from -0.09375 to 0.09375
- first_expand: float32 [512, 2048], P('chan', 'batch'), may hold values from -0.25 to 0.25
- first_shortcut: float32 [1024, 2048], P('batch', 'chan'), may hold values from -0.1875 to 0.1875
- second_reduce: float32 [2048, 512], P('batch', 'chan'), may hold values from -0.125 to 0.125
- second_spatial: float32 [3, 3, 512, 512], P(None, None, 'batch', 'chan'), may hold values from -0.09375 to 0.09375
- second_expand: float32 [512, 2048], P('chan', 'batch'), may hold values from -0.25 to 0.25
- first_mid_gain: float32 [2, 512], P(None, 'chan'), may hold values from 0.5 to 1.5
- first_mid_bias: float32 [2, 512], P(None, 'chan'), may hold values from -2.5 to 2.5
- first_wide_gain: float32 [2, 2048], P(None, 'chan'), may hold values from 0.5 to 1.5
- first_wide_bias: float32 [2, 2048], P(None, 'chan'), may hold values from -2.5 to 2.5
- second_mid_gain: float32 [2, 512], P(None, 'chan'), may hold values from 0.5 to 1.5
- second_mid_bias: float32 [2, 512], P(None, 'chan'), may hold values from -2.5 to 2.5
- second_wide_gain: float32 [2048], P('chan'), may hold values from 0.5 to 1.5
- second_wide_bias: float32 [2048], P('chan'), may hold values from -2.5 to 2.5
- subnet_widths: int32 [3], replicated, may hold values from 256 to 480, as said below
- subnet_ids: int32 [128], replicated, may hold values from 0 to 2, as said below
- crop_sides: int32 [128], replicated, may hold values from 2 to 14, as said below
- cotangent: bfloat16 [128, 7, 7, 2048], P('batch', None, None, 'chan'), may hold values from -6 to 6
Outputs:
- output: float32 [128, 7, 7, 2048], P('batch', None, None, 'chan')
- input_grad: float32 [128, 14, 14, 1024], P('batch', None, None, 'chan')
- first_reduce_grad: float32 [1024, 512], P('batch', 'chan')
- first_spatial_grad: float32 [3, 3, 512, 512], P(None, None, 'batch', 'chan')
- first_expand_grad: float32 [512, 2048], P('chan', 'batch')
- first_shortcut_grad: float32 [1024, 2048], P('batch', 'chan')
- second_reduce_grad: float32 [2048, 512], P('batch', 'chan')
- second_spatial_grad: float32 [3, 3, 512, 512], P(None, None, 'batch', 'chan')
- second_expand_grad: float32 [512, 2048], P('chan', 'batch')
- first_mid_gain_grad: float32 [2, 512], P(None, 'chan')
- first_mid_bias_grad: float32 [2, 512], P(None, 'chan')
- first_wide_gain_grad: float32 [2, 2048], P(None, 'chan')
- first_wide_bias_grad: float32 [2, 2048], P(None, 'chan')
- second_mid_gain_grad: float32 [2, 512], P(None, 'chan')
- second_mid_bias_grad: float32 [2, 512], P(None, 'chan')
- second_wide_gain_grad: float32 [2048], P('chan')
- second_wide_bias_grad: float32 [2048], P('chan')
Inputs may be any that keep to these rules, and one draw needn't show every extreme that they name: `subnet_widths`: multiples of 32; the smallest student has 256 channels and the largest 512 - 512 // 16. `subnet_ids`: every subnet trains at least one crop. `crop_sides`: even; crops 8k and 8k + 1 (an image's two large crops) have 14 - 2 or 14, the six others at most 6.
All inputs are finite; a program needn't handle non-finite values.
Results may differ from a plain program's by a relative error of at most 0.025.
Values may be sent and summed in bfloat16 or wider, within the bound.
No kernel may reach another device: no remote copies, remote signals or barrier semaphores. Data moves between devices by JAX's collectives and lax.ppermute only.
A program may use at most 192 MiB of HBM per device.

v0:
```python
import jax
import jax.numpy as jnp
import numpy as np
from jax import lax
from jax.experimental import pallas as pl
from jax.experimental.pallas import tpu as pltpu
from jax.sharding import PartitionSpec as P

F32, BF16 = jnp.float32, jnp.bfloat16
EPS = 1e-05
SMALL = 6
LANES = 128
ALL = ("batch", "chan")


class Geometry:
    def __init__(self, crops, side):
        self.crops, self.side = crops, side
        self.half, self.small = side // 2, SMALL // 2
        self.large = [c for c in range(crops) if c % 8 < 2]
        grid = [(i, j) for i in range(self.half) for j in range(self.half)]
        self.common = [at for at in grid if max(at) < self.small]
        self.others = [at for at in grid if max(at) >= self.small]
        rows = [(c, i, j) for i, j in self.common for c in range(crops)]
        rows += [(c, i, j) for i, j in self.others for c in self.large]
        self.cut = len(self.common) * crops
        self.rows = np.array(rows, np.int32)
        self.pixels = len(rows)
        where = {tuple(r): n for n, r in enumerate(rows)}
        source = np.full((self.pixels, 16), -1, np.int32)
        for n, (crop, i, j) in enumerate(rows):
            for shift in range(9):
                source[n, shift] = where.get((crop, i + shift // 3 - 1, j + shift % 3 - 1), -1)
        self.source = source
        self.group = 8
        wanted = len(self.large)
        pick = np.zeros((self.group * wanted, self.group * crops), np.float32)
        for n in range(self.group):
            for m, c in enumerate(self.large):
                pick[n * wanted + m, n * crops + c] = 1.0
        self.pick = pick

    def pack(self, pick, load, store):
        for n, (i, j) in enumerate(self.common):
            store(n * self.crops, load(i, j))
        wanted = len(self.large)
        for n in range(0, len(self.others), self.group):
            rows = jnp.concatenate([load(i, j) for i, j in self.others[n : n + self.group]], axis=0)
            store(self.cut + n * wanted, dot(pick, rows).astype(rows.dtype))

    def unpack(self, load, store):
        for n, (i, j) in enumerate(self.common):
            store(i, j, 0, load(n * self.crops, self.crops))
        wanted = len(self.large)
        for n, (i, j) in enumerate(self.others):
            rows = load(self.cut + n * wanted, wanted)
            store(i, j, 0, jnp.zeros((self.crops, rows.shape[1]), rows.dtype))
            for m in range(0, wanted, 2):
                store(i, j, self.large[m], rows[m : m + 2])


UNIT_TAPS = [(0, tap) for tap in range(9)]
STRIDED_TAPS = [
    (2 * int(r != 1) + int(c != 1), 3 * (0 if r == 0 else 1) + (0 if c == 0 else 1))
    for r in range(3)
    for c in range(3)
]
STRIDED_ORDER = [tap for plane in range(4) for tap in range(9) if STRIDED_TAPS[tap][0] == plane]

SM = pl.BlockSpec(memory_space=pltpu.SMEM)


def struct(shape, dtype=F32):
    return jax.ShapeDtypeStruct(tuple(shape), dtype)


def whole_block(shape, at=None):
    at = at or (0,) * len(shape)
    return pl.BlockSpec(tuple(shape), lambda _: at)


def part(array, shape, at):
    return array, whole_block(shape, at)


def corner(array):
    shape = (1,) * (array.ndim - 2) + (16, LANES) if array.ndim > 1 else array.shape
    return array, whole_block([min(a, b) for a, b in zip(shape, array.shape)], (0,) * array.ndim)


def call(kernel, outs, place, *args, flops=10**8, mib=64, after=()):
    args = [a if isinstance(a, tuple) else (a, whole_block(a.shape)) for a in args]
    moved = sum(int(np.prod([n or 1 for n in b.block_shape])) * a.dtype.itemsize for a, b in args)
    moved += sum(int(np.prod(o.shape)) * o.dtype.itemsize for o in outs)
    used, args = len(args), args + [corner(a) for a in after]

    def body(p_ref, *refs):
        kernel(p_ref, *refs[:used], *refs[len(args) :])

    return pl.pallas_call(
        body,
        grid=(1,),
        out_shape=tuple(outs),
        in_specs=[SM] + [b for _, b in args],
        out_specs=tuple(whole_block(o.shape) for o in outs),
        compiler_params=pltpu.CompilerParams(vmem_limit_bytes=mib * 1024 * 1024),
        cost_estimate=pl.CostEstimate(flops=flops, bytes_accessed=moved, transcendentals=0),
    )(place, *[a for a, _ in args])


def dot(a, b):
    return jnp.dot(a, b, preferred_element_type=F32)


def dot_nt(a, b):
    return lax.dot_general(a, b, (((1,), (1,)), ((), ())), preferred_element_type=F32)


def dot_tn(a, b):
    return lax.dot_general(a, b, (((0,), (0,)), ((), ())), preferred_element_type=F32)


def columns_of(seg, subs):
    return [jnp.broadcast_to(seg[:, s : s + 1], (seg.shape[0], LANES)) for s in range(subs)]


def select(seg, rows):
    total = seg[0] * rows[0]
    for s in range(1, len(rows)):
        total = total + seg[s] * rows[s]
    return total


def mask_of(seg):
    mask = seg[0]
    for other in seg[1:]:
        mask = mask + other
    return mask


def sums(seg, field):
    return [jnp.sum(field * g, axis=0, keepdims=True) for g in seg]


def moments(total, count, subs):
    average = [total[s] / count[s] for s in range(subs)]
    inverse = [
        lax.rsqrt(total[subs + s] / count[s] - average[s] * average[s] + EPS) for s in range(subs)
    ]
    return average, inverse


def silu_and_slope(norm):
    sigmoid = jax.nn.sigmoid(norm)
    return norm * sigmoid, sigmoid * (1.0 + norm * (1.0 - sigmoid))


def shifted(source, shift, value):
    if shift == 4:
        return value
    rows = value.shape[0]
    at = lax.broadcasted_iota(jnp.int32, (rows, rows), 1)
    move = jnp.where(at == source[:, shift : shift + 1], 1.0, 0.0).astype(BF16)
    return dot(move, value).astype(BF16)


def put_rows(ref, rows):
    for n, row in enumerate(rows):
        ref[n : n + 1, :] = row


def put_sums(ref, rows, first=0):
    for n, row in enumerate(rows):
        ref[0, first + n : first + n + 1, :] = row


def fan_out(ref):
    block = ref[0]
    for b in range(1, ref.shape[0]):
        ref[b] = block


def whole_tiles(rows):
    return -(-rows // 8) * 8


def block_lanes(k):
    return slice(k * LANES, (k + 1) * LANES)


def row_list(block, first, count):
    return [block[n : n + 1] for n in range(first, first + count)]


def local(
    block_input,
    first_reduce,
    first_spatial,
    first_expand,
    first_shortcut,
    second_reduce,
    second_spatial,
    second_expand,
    first_mid_gain,
    first_mid_bias,
    first_wide_gain,
    first_wide_bias,
    second_mid_gain,
    second_mid_bias,
    second_wide_gain,
    second_wide_bias,
    subnet_widths,
    subnet_ids,
    crop_sides,
    cotangent,
):
    nb, nc = lax.axis_size("batch"), lax.axis_size("chan")
    spread = nb // nc
    crops, side = block_input.shape[0], block_input.shape[1]
    geo = Geometry(crops, side)
    px = geo.pixels
    subs = subnet_widths.shape[0]
    me, ber = lax.axis_index("chan"), lax.axis_index("batch")
    mid = first_reduce.shape[1]
    wide = first_shortcut.shape[1]
    part_in = block_input.shape[3]
    whole_mid = nc * mid
    wide_blocks = wide // LANES

    def chan_swap(x, r):
        return lax.ppermute(x, "chan", [(i, i ^ r) for i in range(nc)])

    def slots_of(x):
        return [x] + [chan_swap(x, r) for r in range(1, nc)]

    def swap_slots(x):
        return [x[0]] + [chan_swap(x[r], r) for r in range(1, nc)]

    def to_batch(x):
        return lax.all_to_all(x, "batch", 0, 0, tiled=True)

    def to_all(x):
        return lax.all_to_all(x, ALL, 0, 0, tiled=True)

    turn = []
    for zc in range(nc):
        for j in range(spread):
            for c in range(nc):
                turn.append(((zc * spread + j) * nc + c, (c * spread + j) * nc + zc))

    def turn_share(x):
        return lax.ppermute(x, ALL, turn)

    s_rows, e_cols, r2_rows = first_spatial.shape[2], first_expand.shape[1], second_reduce.shape[0]
    in_rows, part_in = first_reduce.shape[0], block_input.shape[3]
    early = 2

    def prepare_kernel(
        p_ref, x_ref, pick_ref, r1_ref, s1_ref, e1_ref, sc_ref, r2_ref, s2_ref, e2_ref,
        entry_ref, first_out, later_out, turn_out, mine_out, s2_out,
    ):
        picked = pick_ref[...]
        for k in range(4):

            def store(first, rows):
                entry_ref[k, first : first + rows.shape[0], :] = rows

            geo.pack(picked, lambda i, j: x_ref[2 * i + k // 2, 2 * j + k % 2], store)
        r1, s1 = r1_ref[...].astype(BF16), s1_ref[...].astype(BF16)
        for b in range(nb):
            first_out[b, 0:in_rows] = r1
            first_out[b, in_rows:] = s1[: early * s_rows]
            later_out[b] = s1[early * s_rows :]
        s2_out[...] = s2_ref[...].astype(BF16)
        turn_out[0:e_cols] = e1_ref[...].T.astype(BF16)
        turn_out[e_cols : e_cols + r2_rows] = r2_ref[...].astype(BF16)
        turn_out[e_cols + r2_rows :] = e2_ref[...].T.astype(BF16)
        for k in range(wide_blocks):
            mine_out[k * in_rows : (k + 1) * in_rows] = sc_ref[:, block_lanes(k)].astype(BF16)

    def gather_batch(x):
        return lax.all_gather(x, "batch", axis=0, tiled=False)

    place = jnp.stack([me, ber]).astype(jnp.int32)
    pick_large = jnp.asarray(geo.pick, BF16)
    b_rows, turn_rows = e_cols + r2_rows + wide_blocks * in_rows, 2 * e_cols + r2_rows
    entry, first, later, turned, mine, s2_rows = call(
        prepare_kernel,
        (
            struct((4, px, part_in), BF16),
            struct((nb, in_rows + early * s_rows, mid), BF16),
            struct((nb, (9 - early) * s_rows, mid), BF16),
            struct((turn_rows, mid), BF16),
            struct((wide_blocks * in_rows, mid), BF16),
            struct((9 * s_rows, mid), BF16),
        ),
        place, block_input.transpose(1, 2, 0, 3), pick_large, first_reduce, first_spatial.reshape(9 * s_rows, mid),
        first_expand, first_shortcut, second_reduce, second_spatial.reshape(9 * s_rows, mid), second_expand,
    )
    entry = lax.all_gather(entry, "chan", axis=0, tiled=False)
    entries = [part(entry, (None, 4, px, part_in), (c, 0, 0, 0)) for c in range(nc)]
    first, later, turned = to_batch(first), to_batch(later), turn_share(turned)
    r1_w = part(first, (nb, in_rows, mid), (0, 0, 0))

    def shares_kernel(p_ref, turned_ref, mine_ref, s2_ref, b_out, c_out):
        b_out[0 : e_cols + r2_rows] = turned_ref[0 : e_cols + r2_rows]
        b_out[e_cols + r2_rows :] = mine_ref[...]
        c_out[0:e_cols] = turned_ref[e_cols + r2_rows :]
        c_out[e_cols:] = s2_ref[...]

    b_share, c_share = call(
        shares_kernel,
        (struct((b_rows, mid), BF16), struct((e_cols + 9 * s_rows, mid), BF16)),
        place, turned, mine, s2_rows, after=[first],
    )
    group_b, group_c = gather_batch(b_share), gather_batch(c_share)
    e1_w = part(group_b, (nb, e_cols, mid), (0, 0, 0))
    r2_w = part(group_b, (nb, r2_rows, mid), (0, e_cols // r2_rows, 0))
    sc_w = part(group_b, (nb, wide_blocks * in_rows, mid), (0, (e_cols + r2_rows) // (wide_blocks * in_rows), 0))
    e2_w = part(group_c, (nb, e_cols, mid), (0, 0, 0))

    def spatial_weight(x, at):
        rows, per = s_rows, spread
        if s_rows % 16:
            x = x[:, at:].reshape(nc, spread, 9, s_rows, mid).transpose(0, 2, 1, 3, 4)
            x, at, rows, per = x.reshape(nc, 9 * mid, mid), 0, mid, 1
        return [part(x, (x.shape[0], rows, mid), (0, at // rows + tap, 0)) for tap in range(9)], per

    if s_rows % 16:
        s1_w = spatial_weight(jnp.concatenate([first[:, in_rows:], later], axis=1), 0)
    else:
        one, two = spatial_weight(first, in_rows), spatial_weight(later, -early * s_rows)
        s1_w = one[0][:early] + two[0][early:], spread
    s2_w = spatial_weight(group_c, e_cols)

    start = ber * crops
    sides = lax.dynamic_slice_in_dim(crop_sides, start, crops)
    ids = lax.dynamic_slice_in_dim(subnet_ids, start, crops)
    labels = jnp.arange(8, dtype=jnp.int32)
    member_all = (subnet_ids[None, :] == labels[:subs, None]).astype(F32)
    halves = crop_sides // 2
    count_full = jnp.sum(member_all * (crop_sides * crop_sides).astype(F32)[None, :], axis=1)
    count_half = jnp.sum(member_all * (halves * halves).astype(F32)[None, :], axis=1)
    counts = jnp.broadcast_to(
        jnp.concatenate([count_half, count_full, jnp.ones((8 - 2 * subs,), F32)])[:, None], (8, LANES)
    )
    pick = jnp.asarray(geo.rows[:, 0:1] == np.arange(crops)[None, :])
    side_row = jnp.sum(jnp.where(pick, sides[None, :], 0), axis=1, keepdims=True)
    id_row = jnp.sum(jnp.where(pick, ids[None, :], 0), axis=1, keepdims=True)
    row_i, row_j = jnp.asarray(geo.rows[:, 1:2]), jnp.asarray(geo.rows[:, 2:3])
    own = id_row == labels[None, :]
    seg_half = (own & (row_i < side_row // 2) & (row_j < side_row // 2)).astype(F32)
    seg_full = jnp.stack(
        [
            (own & (2 * row_i + p < side_row) & (2 * row_j + q < side_row)).astype(F32)
            for p in range(2)
            for q in range(2)
        ]
    )
    channel = jnp.arange(whole_mid, dtype=jnp.int32).reshape(nc, 1, mid)
    limits = jnp.concatenate([subnet_widths, jnp.zeros((8 - subs,), jnp.int32)])
    active = (channel < limits[None, :, None]).astype(F32)
    source = jnp.asarray(geo.source)
    own_params = jnp.concatenate([first_mid_gain, first_mid_bias, second_mid_gain, second_mid_bias], axis=0)
    params = jnp.stack(slots_of(own_params))

    def norm_slots(p_ref, raw, st_ref, par_ref, active_ref, seg, count, which, put, keep_slot):
        block, layer = which
        chan = p_ref[0]
        for r in range(nc):
            ch = chan ^ r
            total = st_ref[ch]
            for b in range(1, nb):
                total = total + st_ref[b * nc + ch]
            average, inverse = moments(row_list(total, 0, 2 * subs), count, subs)
            gain = par_ref[r, 4 * block + layer : 4 * block + layer + 1, :]
            bias = par_ref[r, 4 * block + 2 + layer : 4 * block + 3 + layer, :]
            act_rows = row_list(active_ref[ch], 0, subs)
            xhat = (raw(r).astype(F32) - select(seg, average)) * select(seg, inverse)
            keep = select(seg, act_rows)
            value, slope = silu_and_slope(gain * xhat + bias)
            put(r, (value * keep).astype(BF16))
            keep_slot(r, xhat, slope * keep, inverse)

    def send_sums(st_ref, seg, raw):
        value = raw.astype(F32)
        put_sums(st_ref, sums(seg, value) + sums(seg, value * value))
        fan_out(st_ref)

    every = nb * nc

    def joined(ref, *at):
        return jnp.concatenate([ref[(*at, r)] for r in range(nc)], axis=1)

    def block_rows(p_ref, ref, r):
        return jnp.concatenate([ref[(p_ref[0] ^ r) * spread + j] for j in range(spread)], axis=0)

    def joined_weight(p_ref, ref):
        return jnp.concatenate([block_rows(p_ref, ref, r) for r in range(nc)], axis=1)

    def tap_weight(p_ref, ref, per):
        return jnp.concatenate([ref[(p_ref[0] ^ r) * per + j] for r in range(nc) for j in range(per)], axis=0)

    def reduce_rows(ref, c):
        return jnp.concatenate([ref[c * spread + j] for j in range(spread)], axis=0)

    def shortcut_rows(ref, c):
        return jnp.concatenate(
            [
                jnp.concatenate(
                    [ref[c * spread + j, k * in_rows : (k + 1) * in_rows, :] for k in range(wide_blocks)], axis=1
                )
                for j in range(spread)
            ],
            axis=0,
        )

    def reduce_kernel(p_ref, e0, e1_, e2_, e3, w_ref, seg_ref, raw_ref, st_ref):
        w = jnp.concatenate([reduce_rows(w_ref, c) for c in range(nc)], axis=0)
        rows = [jnp.zeros((1, LANES), F32)] * (2 * subs)
        for k in range(4):
            seg = columns_of(seg_ref[k], subs)
            mask = mask_of(seg)
            raw = (dot(jnp.concatenate([e[k] for e in (e0, e1_, e2_, e3)], axis=1), w) * mask).astype(BF16)
            raw_ref[k] = raw
            value = raw.astype(F32)
            new = sums(seg, value) + sums(seg, value * value)
            rows = [a + b for a, b in zip(rows, new)]
        put_sums(st_ref, rows)
        fan_out(st_ref)

    def short_kernel(p_ref, e0, e1_, e2_, e3, w_ref, segh_ref, out_ref):
        w = jnp.concatenate([shortcut_rows(w_ref, c) for c in range(nc)], axis=0)
        got = dot(jnp.concatenate([e[...] for e in (e0, e1_, e2_, e3)], axis=1), w)
        out_ref[...] = got * jnp.sum(segh_ref[...], axis=1, keepdims=True)

    def spatial_one_kernel(
        p_ref, r0, r1_, r2_, r3, st_ref, par_ref, act_ref, segf_ref, segh_ref, cnt_ref, src_ref, *rest
    ):
        w_refs, (out_ref, xhat_ref, slope_ref, inv_ref, raw_ref, sto_ref) = rest[:9], rest[9:]
        refs = (r0, r1_, r2_, r3)
        count = row_list(cnt_ref[...], subs, subs)
        for k in range(4):
            seg = columns_of(segf_ref[k], subs)

            def put(r, value):
                out_ref[k, r] = value

            def keep_slot(r, xhat, slope, inverse):
                xhat_ref[r, k] = xhat.astype(BF16)
                slope_ref[r, k] = slope.astype(BF16)
                if k == 0 and r == 0:
                    put_rows(inv_ref, inverse)

            norm_slots(
                p_ref, lambda r: refs[r][k], st_ref, par_ref, act_ref, seg, count, (0, 0), put, keep_slot
            )
        src = src_ref[...]
        total = jnp.zeros((px, mid), F32)
        for tap in range(9):
            plane, shift = STRIDED_TAPS[tap]
            total = total + dot(shifted(src, shift, joined(out_ref, plane)), tap_weight(p_ref, w_refs[tap], s1_w[1]))
        raw = total.astype(BF16)
        raw_ref[...] = raw
        send_sums(sto_ref, columns_of(segh_ref[...], subs), raw)

    def mid_inputs(raws, st):
        return (*raws, st, params, active, seg_half, counts)

    def mid_outs():
        return (
            struct((nc, px, mid), BF16),
            struct((nc, px, mid)),
            struct((nc, px, mid)),
            struct((8, mid)),
        )

    def mid_part(which, p_ref, refs, st_ref, par_ref, act_ref, segh_ref, cnt_ref, out_ref, xhat_ref, slope_ref, inv_ref):
        seg = columns_of(segh_ref[...], subs)

        def put(r, value):
            out_ref[r] = value

        def keep_slot(r, xhat, slope, inverse):
            xhat_ref[r] = xhat
            slope_ref[r] = slope
            if r == 0:
                put_rows(inv_ref, inverse)

        norm_slots(
            p_ref, lambda r: refs[r][...], st_ref, par_ref, act_ref, seg,
            row_list(cnt_ref[...], 0, subs), which, put, keep_slot,
        )
        return seg

    def wide_sums(st_ref, seg, fields):
        for k in range(wide_blocks):
            rows = fields(k)
            put_sums(st_ref, rows, k * len(rows))
        fan_out(st_ref)

    def expand_one_kernel(
        p_ref, r0, r1_, r2_, r3, st_ref, par_ref, act_ref, segh_ref, cnt_ref, w_ref, short_ref,
        out_ref, xhat_ref, slope_ref, inv_ref, pre_ref, sto_ref,
    ):
        seg = mid_part(
            (0, 1), p_ref, (r0, r1_, r2_, r3), st_ref, par_ref, act_ref, segh_ref, cnt_ref,
            out_ref, xhat_ref, slope_ref, inv_ref,
        )
        pre_ref[...] = dot_nt(joined(out_ref), joined_weight(p_ref, w_ref))

        def fields(k):
            a, b = pre_ref[:, block_lanes(k)], short_ref[:, block_lanes(k)]
            return sums(seg, a) + sums(seg, a * a) + sums(seg, b) + sums(seg, b * b)

        wide_sums(sto_ref, seg, fields)

    def summed(st_ref, k=0, rows=2 * subs):
        total = st_ref[0, k * rows : (k + 1) * rows, :]
        for b in range(1, nb):
            total = total + st_ref[b, k * rows : (k + 1) * rows, :]
        return total

    def to_slots(slot_refs, value):
        for r in range(nc):
            slot_refs[r][...] = value[:, r * mid : (r + 1) * mid].astype(BF16)

    def send_upstream(p_ref, slot_refs, st_ref, seg, back, slope_ref, xhat_ref):
        for r in range(nc):
            u = (back[:, r * mid : (r + 1) * mid] * slope_ref[r]).astype(BF16)
            slot_refs[r][...] = u
            u = u.astype(F32)
            send_block(p_ref, st_ref, r, sums(seg, u) + sums(seg, u * xhat_ref[r]))

    def send_block(p_ref, st_ref, r, rows):
        block = jnp.concatenate(rows + [jnp.zeros((8 - len(rows), LANES), F32)], axis=0)
        for b in range(nb):
            st_ref[b * nc + (p_ref[0] ^ r)] = block

    def received(refs, *at):
        total = refs[0][at or ...].astype(F32)
        for ref in refs[1:]:
            total = total + ref[at or ...].astype(F32)
        return total

    def all_summed(st_ref):
        total = st_ref[0]
        for b in range(1, every):
            total = total + st_ref[b]
        return total

    def section_kernel(
        p_ref, st_ref, three_ref, short_ref, gain_ref, bias_ref, segh_ref, cnt_ref, w_ref,
        xh3_ref, xhs_ref, out_ref, slope_ref, inv_ref, low_ref, *slot_refs,
    ):
        seg = columns_of(segh_ref[...], subs)
        mask = mask_of(seg)
        count = row_list(cnt_ref[...], 0, subs)
        for k in range(wide_blocks):
            ln = block_lanes(k)
            total = summed(st_ref, k, 4 * subs)
            both = None
            for n, (pre, keep) in enumerate(((three_ref, xh3_ref), (short_ref, xhs_ref))):
                average, inverse = moments(row_list(total, 2 * subs * n, 2 * subs), count, subs)
                xhat = (pre[:, ln] - select(seg, average)) * select(seg, inverse)
                keep[:, ln] = xhat
                for s in range(subs):
                    inv_ref[n * subs + s : n * subs + s + 1, ln] = inverse[s]
                norm = gain_ref[n : n + 1, ln] * xhat + bias_ref[n : n + 1, ln]
                both = norm if both is None else both + norm
            value, slope = silu_and_slope(both)
            value = value * mask
            out_ref[:, ln] = value
            slope_ref[:, ln] = slope * mask
            low_ref[:, ln] = value.astype(BF16)
        to_slots(slot_refs, dot(low_ref[...], joined_weight(p_ref, w_ref)))

    def four_kernel(p_ref, s0, s1_, s2_, s3, segh_ref, raw_ref, sto_ref):
        total = s0[...].astype(F32)
        for ref in (s1_, s2_, s3):
            total = total + ref[...].astype(F32)
        raw = total.astype(BF16)
        raw_ref[...] = raw
        send_sums(sto_ref, columns_of(segh_ref[...], subs), raw)

    def spatial_two_kernel(
        p_ref, r0, r1_, r2_, r3, st_ref, par_ref, act_ref, segh_ref, cnt_ref, src_ref, *rest
    ):
        w_refs, (out_ref, xhat_ref, slope_ref, inv_ref, raw_ref, sto_ref) = rest[:9], rest[9:]
        seg = mid_part(
            (1, 0), p_ref, (r0, r1_, r2_, r3), st_ref, par_ref, act_ref, segh_ref, cnt_ref,
            out_ref, xhat_ref, slope_ref, inv_ref,
        )
        src = src_ref[...]
        total = jnp.zeros((px, mid), F32)
        whole = joined(out_ref)
        for tap in range(9):
            total = total + dot(shifted(src, tap, whole), tap_weight(p_ref, w_refs[tap], s2_w[1]))
        raw = total.astype(BF16)
        raw_ref[...] = raw
        send_sums(sto_ref, seg, raw)

    def expand_two_kernel(
        p_ref, r0, r1_, r2_, r3, st_ref, par_ref, act_ref, segh_ref, cnt_ref, w_ref,
        out_ref, xhat_ref, slope_ref, inv_ref, pre_ref, sto_ref,
    ):
        seg = mid_part(
            (1, 1), p_ref, (r0, r1_, r2_, r3), st_ref, par_ref, act_ref, segh_ref, cnt_ref,
            out_ref, xhat_ref, slope_ref, inv_ref,
        )
        pre_ref[...] = dot_nt(joined(out_ref), joined_weight(p_ref, w_ref))

        def fields(k):
            a = pre_ref[:, block_lanes(k)]
            return sums(seg, a) + sums(seg, a * a)

        wide_sums(sto_ref, seg, fields)

    def final_kernel(
        p_ref, st_ref, pre_ref, section_ref, cot_ref, gain_ref, bias_ref, segh_ref, cnt_ref, pick_ref,
        out_ref, grad_ref, xhat_ref, inv_ref, sto_ref,
    ):
        seg = columns_of(segh_ref[...], subs)
        mask = mask_of(seg)
        count = row_list(cnt_ref[...], 0, subs)
        picked = pick_ref[...]
        for k in range(wide_blocks):
            ln = block_lanes(k)
            average, inverse = moments(row_list(summed(st_ref, k), 0, 2 * subs), count, subs)
            xhat = (pre_ref[:, ln] - select(seg, average)) * select(seg, inverse)
            xhat_ref[:, ln] = xhat
            for s in range(subs):
                inv_ref[s : s + 1, ln] = inverse[s]
            both = gain_ref[:, ln] * xhat + bias_ref[:, ln] + section_ref[:, ln]
            value, slope = silu_and_slope(both)
            value = value * mask

            def place_out(i, j, first, rows):
                out_ref[i, j, first : first + rows.shape[0], ln] = rows

            geo.unpack(lambda first, count: value[first : first + count], place_out)
            parts = []
            geo.pack(picked, lambda i, j: cot_ref[i, j, :, ln], lambda first, rows: parts.append(rows))
            grad = jnp.concatenate(parts, axis=0).astype(F32) * mask * slope
            grad_ref[:, ln] = grad
            put_sums(sto_ref, sums(seg, grad) + sums(seg, grad * xhat), k * 2 * subs)
        fan_out(sto_ref)

    def norm_back(total, at, gain, inverse, u, xhat, seg, count):
        g = [total[s : s + 1] / count[s] for s in range(subs)]
        x = [total[at + s : at + s + 1] / count[s] for s in range(subs)]
        scale = select(seg, [gain * row for row in inverse])
        return (scale * (u - (select(seg, g) + xhat * select(seg, x)))).astype(BF16)

    def put_param_grads(ref, ln, total, pairs):
        for n, first in enumerate(pairs):
            row = total[first : first + 1]
            for s in range(1, subs):
                row = row + total[first + s : first + s + 1]
            ref[n : n + 1, ln] = row

    def back_six_kernel(
        p_ref, st_ref, u_ref, xhat_ref, inv_ref, gain_ref, segh_ref, cnt_ref, w_ref, slope_ref, xh5_ref, low_ref, par_ref, sto_ref, *slot_refs
    ):
        seg = columns_of(segh_ref[...], subs)
        count = row_list(cnt_ref[...], 0, subs)
        for k in range(wide_blocks):
            ln = block_lanes(k)
            total = summed(st_ref, k)
            put_param_grads(par_ref, ln, total, (subs, 0))
            low_ref[:, ln] = norm_back(
                total, subs, gain_ref[:, ln], row_list(inv_ref[:, ln], 0, subs), u_ref[:, ln], xhat_ref[:, ln], seg, count
            )
        send_upstream(p_ref, slot_refs, sto_ref, seg, dot(low_ref[...], joined_weight(p_ref, w_ref)), slope_ref, xh5_ref)

    def own_gain(ref, which):
        block, layer = which
        return ref[0, 4 * block + layer : 4 * block + layer + 1, :]

    def back_own(st_ref, u_refs, xhat_ref, inv_ref, params_ref, which, segh_ref, cnt_ref, par_ref):
        seg = columns_of(segh_ref[...], subs)
        total = all_summed(st_ref)
        put_param_grads(par_ref, slice(0, LANES), total, (subs, 0))
        return seg, norm_back(
            total, subs, own_gain(params_ref, which), row_list(inv_ref[...], 0, subs), received(u_refs), xhat_ref[...],
            seg, row_list(cnt_ref[...], 0, subs),
        )

    def back_spatial_kernel(which, taps, order, per, with_grads):
        def kernel(
            p_ref, st_ref, u0, u1, u2, u3, xhat_ref, inv_ref, params_ref, segh_ref, cnt_ref, src_ref,
            slope_ref, xhats_ref, segs_ref, *rest
        ):
            w_refs, rest = rest[:9], rest[9:]
            if with_grads:
                act_ref, keep_ref, send_ref, par_ref, sto_ref, *slot_refs = rest
            else:
                cols_ref, par_ref, sto_ref, *slot_refs = rest
            shifts = []
            _, low = back_own(
                st_ref, (u0, u1, u2, u3), xhat_ref, inv_ref, params_ref, which, segh_ref, cnt_ref, par_ref
            )
            src = src_ref[...]
            rows = [None] * nc
            back = None
            for n, tap in enumerate(order):
                plane, shift = taps[tap]
                g = shifted(src, 8 - shift, low)
                shifts.append(g)
                if not with_grads:
                    cols_ref[:, n * mid : (n + 1) * mid] = g
                new = dot_nt(g, tap_weight(p_ref, w_refs[tap], per))
                back = new if back is None else back + new
                if n < 8 and taps[order[n + 1]][0] == plane:
                    continue
                seg = columns_of(segs_ref[plane], subs)
                for r in range(nc):
                    u = (back[:, r * mid : (r + 1) * mid] * slope_ref[r, plane].astype(F32)).astype(BF16)
                    slot_refs[r][plane] = u
                    u = u.astype(F32)
                    got = sums(seg, u) + sums(seg, u * xhats_ref[r, plane].astype(F32))
                    rows[r] = got if rows[r] is None else [a + b for a, b in zip(rows[r], got)]
                back = None
            for r in range(nc):
                send_block(p_ref, sto_ref, r, rows[r])
            if with_grads:
                put_strided(p_ref, act_ref, shifts, keep_ref, send_ref)

        return kernel

    def back_plain_kernel(which):
        def kernel(p_ref, st_ref, u0, u1, u2, u3, xhat_ref, inv_ref, params_ref, segh_ref, cnt_ref, low_ref, par_ref):
            _, low_ref[...] = back_own(
                st_ref, (u0, u1, u2, u3), xhat_ref, inv_ref, params_ref, which, segh_ref, cnt_ref, par_ref
            )

        return kernel

    def back_section_kernel(
        p_ref, g0, g1, g2, g3, w_ref, grad_ref, slope_ref, xh3_ref, xhs_ref, segh_ref,
        whole_ref, u_ref, sto_ref,
    ):
        for r, ref in enumerate((g0, g1, g2, g3)):
            whole_ref[r] = ref[...]
        u_ref[...] = dot_nt(joined(whole_ref), joined_weight(p_ref, w_ref))
        seg = columns_of(segh_ref[...], subs)
        for k in range(wide_blocks):
            ln = block_lanes(k)
            u = (u_ref[:, ln] + grad_ref[:, ln]) * slope_ref[:, ln]
            u_ref[:, ln] = u
            rows = sums(seg, u) + sums(seg, u * xh3_ref[:, ln]) + sums(seg, u * xhs_ref[:, ln])
            put_sums(sto_ref, rows, k * 3 * subs)
        fan_out(sto_ref)

    def back_wide_kernel(
        p_ref, st_ref, u_ref, xh3_ref, xhs_ref, inv_ref, gain_ref, segh_ref, cnt_ref, w_ref, slope_ref, xh2_ref,
        three_ref, short_ref, par_ref, sto_ref, *slot_refs,
    ):
        seg = columns_of(segh_ref[...], subs)
        count = row_list(cnt_ref[...], 0, subs)
        for k in range(wide_blocks):
            ln = block_lanes(k)
            total = summed(st_ref, k, 3 * subs)
            put_param_grads(par_ref, ln, total, (subs, 2 * subs, 0))
            u = u_ref[:, ln]
            inverse = inv_ref[:, ln]
            three_ref[:, ln] = norm_back(
                total, subs, gain_ref[0:1, ln], row_list(inverse, 0, subs), u, xh3_ref[:, ln], seg, count
            )
            short_ref[:, ln] = norm_back(
                total, 2 * subs, gain_ref[1:2, ln], row_list(inverse, subs, subs), u, xhs_ref[:, ln], seg, count
            )
        send_upstream(p_ref, slot_refs, sto_ref, seg, dot(three_ref[...], joined_weight(p_ref, w_ref)), slope_ref, xh2_ref)

    def back_one_kernel(
        p_ref, st_ref, u0, u1, u2, u3, xhat_ref, inv_ref, params_ref, segf_ref, cnt_ref, w_ref, short_ref, sc_ref,
        low_ref, par_ref, *slot_refs,
    ):
        count = row_list(cnt_ref[...], subs, subs)
        total = all_summed(st_ref)
        put_param_grads(par_ref, slice(0, LANES), total, (subs, 0))
        for k in range(4):
            seg = columns_of(segf_ref[k], subs)
            low_ref[k] = norm_back(
                total, subs, own_gain(params_ref, (0, 0)), row_list(inv_ref[...], 0, subs),
                received((u0, u1, u2, u3), k), xhat_ref[k].astype(F32), seg, count,
            )
        for r in range(nc):
            w = reduce_rows(w_ref, p_ref[0] ^ r)
            for k in range(4):
                got = dot_nt(low_ref[k], w)
                if k == 0:
                    got = got + dot_nt(short_ref[...], shortcut_rows(sc_ref, p_ref[0] ^ r))
                slot_refs[r][k] = got.astype(BF16)

    def input_kernel(p_ref, a_ref, b_ref, c_ref, segf_ref, out_ref):
        for k in range(4):
            mask = jnp.sum(segf_ref[k], axis=1, keepdims=True)
            total = a_ref[k].astype(F32) + b_ref[k].astype(F32) + c_ref[k].astype(F32)
            total = total * mask

            def place_out(i, j, first, rows):
                out_ref[2 * i + k // 2, 2 * j + k % 2, first : first + rows.shape[0], :] = rows

            geo.unpack(lambda first, count: total[first : first + count], place_out)

    def put_expand(p_ref, out_ref, at, grad_ref, act_ref):
        for k in range(nc):
            got = dot_tn(grad_ref[...], act_ref[p_ref[0] ^ k]).astype(BF16)
            for j in range(spread):
                out_ref[k * spread + j, at : at + e_cols, :] = got[j * e_cols : (j + 1) * e_cols]

    def put_spatial(out_ref, at, k, taps, got):
        for j in range(spread):
            for n, tap in enumerate(taps):
                first = at + tap * s_rows
                out_ref[k * spread + j, first : first + s_rows, :] = got[
                    j * s_rows : (j + 1) * s_rows, n * mid : (n + 1) * mid
                ]

    def grads_two_kernel(p_ref, six_ref, act5_ref, act4_ref, cols_ref, out_ref):
        put_expand(p_ref, out_ref, 0, six_ref, act5_ref)
        for k in range(nc):
            got = dot_tn(act4_ref[p_ref[0] ^ k], cols_ref[...]).astype(BF16)
            put_spatial(out_ref, e_cols, k, range(9), got)

    def grads_mixed_kernel(p_ref, low_ref, four_ref, three_ref, act2_ref, e0, e1_, e2_, e3, short_ref, out_ref):
        for k in range(nc):
            got = dot_tn(low_ref[...], four_ref[p_ref[0] ^ k]).astype(BF16)
            for j in range(spread):
                out_ref[k * spread + j, 0:r2_rows, :] = got[j * r2_rows : (j + 1) * r2_rows]
        put_expand(p_ref, out_ref, r2_rows, three_ref, act2_ref)
        first = r2_rows + e_cols
        for c, entry_ref in enumerate((e0, e1_, e2_, e3)):
            got = dot_tn(entry_ref[...], short_ref[...]).astype(BF16)
            for j in range(spread):
                for k in range(wide_blocks):
                    out_ref[c * spread + j, first + k * in_rows : first + (k + 1) * in_rows, :] = got[
                        j * in_rows : (j + 1) * in_rows, block_lanes(k)
                    ]

    def grads_reduce_kernel(p_ref, e0, e1_, e2_, e3, grad_ref, out_ref):
        for c, entry_ref in enumerate((e0, e1_, e2_, e3)):
            got = dot_tn(entry_ref[0], grad_ref[0])
            for k in range(1, 4):
                got = got + dot_tn(entry_ref[k], grad_ref[k])
            for j in range(spread):
                out_ref[c * spread + j] = got[j * in_rows : (j + 1) * in_rows].astype(BF16)

    def put_strided(p_ref, act_ref, shifts, keep_ref, send_ref):
        odd = lax.rem(p_ref[1], 2) == 1
        for k in range(nc):
            first = 0
            for plane in range(4):
                taps = [t for t in STRIDED_ORDER if STRIDED_TAPS[t][0] == plane]
                cols = jnp.concatenate(shifts[first : first + len(taps)], axis=1)
                first += len(taps)
                got = dot_tn(act_ref[plane, p_ref[0] ^ k], cols)
                for j in range(0, spread, 2):
                    one, two = got[j * s_rows : (j + 1) * s_rows], got[(j + 1) * s_rows : (j + 2) * s_rows]
                    keep, send = jnp.where(odd, two, one).astype(BF16), jnp.where(odd, one, two).astype(BF16)
                    for n, tap in enumerate(taps):
                        rows = slice(tap * s_rows, (tap + 1) * s_rows)
                        keep_ref[(k * spread + j) // 2, rows, :] = keep[:, block_lanes(n)]
                        send_ref[(k * spread + j) // 2, rows, :] = send[:, block_lanes(n)]

    def mine(p_ref, pair_ref, got_ref):
        return pair_ref[lax.rem(p_ref[1], 2)].astype(F32) + got_ref[...].astype(F32)

    def total_kernel(p_ref, *refs):
        total = refs[0][...].astype(F32)
        for ref in refs[1:-1]:
            total = total + ref[...].astype(F32)
        refs[-1][...] = total.astype(refs[-1].dtype)

    def turn_kernel(p_ref, two_ref, two_got, mixed_ref, mixed_got, turn_out, s2_out, sc_out):
        two, mixed = mine(p_ref, two_ref, two_got), mine(p_ref, mixed_ref, mixed_got)
        turn_out[0:e_cols] = mixed[r2_rows : r2_rows + e_cols].astype(BF16)
        turn_out[e_cols : e_cols + r2_rows] = mixed[0:r2_rows].astype(BF16)
        turn_out[e_cols + r2_rows :] = two[0:e_cols].astype(BF16)
        s2_out[...] = two[e_cols:]
        first = r2_rows + e_cols
        for k in range(wide_blocks):
            sc_out[:, block_lanes(k)] = mixed[first + k * in_rows : first + (k + 1) * in_rows]

    def param_kernel(p_ref, one, two, wide_one, four, five, six, g1, b1, gw1, bw1, g2, b2, gw2, bw2):
        for first, second, gain, bias in ((one, two, g1, b1), (four, five, g2, b2)):
            for n, ref in enumerate((first, second)):
                gain[n : n + 1, :] = ref[0:1, :]
                bias[n : n + 1, :] = ref[1:2, :]
        gw1[...] = wide_one[0:2, :]
        bw1[0:1, :] = wide_one[2:3, :]
        bw1[1:2, :] = wide_one[2:3, :]
        gw2[...] = six[0:1, :]
        bw2[...] = six[1:2, :]

    def own_kernel(p_ref, turned_ref, one_ref, reduce_ref, e1_out, r2_out, e2_out, s1_out, r1_out):
        s1_out[...] = one_ref[...].astype(F32)
        total = reduce_ref[0].astype(F32)
        for b in range(1, nb):
            total = total + reduce_ref[b].astype(F32)
        r1_out[...] = total
        e1_out[...] = turned_ref[0:e_cols].astype(F32).T
        r2_out[...] = turned_ref[e_cols : e_cols + r2_rows].astype(F32)
        e2_out[...] = turned_ref[e_cols + r2_rows :].astype(F32).T

    def to_owners(shares):
        rows = shares.shape[1]
        groups = [list(range(first, nb, 2)) for first in range(2)]
        pair = lax.psum_scatter(
            shares.reshape(nb // 2, 2 * rows, mid), "batch", scatter_dimension=0, axis_index_groups=groups, tiled=False
        ).reshape(2, rows, mid)
        send = lax.dynamic_index_in_dim(pair, 1 - ber % 2, 0, False)
        return pair, lax.ppermute(send, "batch", [(i, i ^ 1) for i in range(nb)])

    st_mid, st_own, st_wide = (
        struct((every, 8, LANES)),
        struct((nb, 8, LANES)),
        struct((nb, whole_tiles(2 * subs * wide_blocks), LANES)),
    )
    matmul = 2 * px * whole_mid * wide
    mid_slots = [struct((px, mid), BF16)] * nc
    half = side // 2

    raw_one, st = call(
        reduce_kernel, (struct((4, px, mid), BF16), st_mid), place, *entries, r1_w, seg_full, flops=4 * matmul
    )
    (st,) = call(total_kernel, (st_mid,), place, st, after=[later])
    raws, st = slots_of(raw_one), to_all(st)
    act_one, xhat_one, slope_one, inv_one, raw_two, st = call(
        spatial_one_kernel,
        (
            struct((4, nc, px, mid), BF16),
            struct((nc, 4, px, mid), BF16),
            struct((nc, 4, px, mid), BF16),
            struct((8, mid)),
            struct((px, mid), BF16),
            st_mid,
        ),
        place, *raws, st, params, active, seg_full, seg_half, counts, source, *s1_w[0],
        flops=10 * matmul,
    )
    shorts = [part(entry, (None, None, px, part_in), (c, 0, 0, 0)) for c in range(nc)]
    (pre_short,) = call(short_kernel, (struct((px, wide)),), place, *shorts, sc_w, seg_half, flops=4 * matmul)
    raws, st = slots_of(raw_two), to_all(st)
    act_two, xhat_two, slope_two, inv_two, pre_three, st = call(
        expand_one_kernel,
        (*mid_outs(), struct((px, wide)), struct((nb, whole_tiles(4 * subs * wide_blocks), LANES))),
        place, *mid_inputs(raws, st), e1_w, pre_short,
        flops=2 * matmul,
    )
    xhat_three, xhat_short, section_out, slope_section, inv_wide, section_low, *slots = call(
        section_kernel,
        (
            *[struct((px, wide))] * 4,
            struct((8, wide)),
            struct((px, wide), BF16),
            *mid_slots,
        ),
        place, to_batch(st), pre_three, pre_short, first_wide_gain, first_wide_bias, seg_half, counts, r2_w,
        flops=2 * matmul,
    )

    raw_four, st = call(
        four_kernel, (struct((px, mid), BF16), st_mid), place, *swap_slots(slots), seg_half
    )
    raws, st = slots_of(raw_four), to_all(st)
    act_four, xhat_four, slope_four, inv_four, raw_five, st = call(
        spatial_two_kernel,
        (*mid_outs(), struct((px, mid), BF16), st_mid),
        place, *mid_inputs(raws, st), source, *s2_w[0],
        flops=8 * matmul,
    )
    raws, st = slots_of(raw_five), to_all(st)
    act_five, xhat_five, slope_five, inv_five, pre_six, st = call(
        expand_two_kernel,
        (*mid_outs(), struct((px, wide)), st_wide),
        place, *mid_inputs(raws, st), e2_w,
        flops=2 * matmul,
    )
    gain_six, bias_six = second_wide_gain[None], second_wide_bias[None]
    out_rows, grad_final, xhat_six, inv_six, st = call(
        final_kernel,
        (struct((half, half, crops, wide)), *[struct((px, wide))] * 2, struct((8, wide)), st_wide),
        place, to_batch(st), pre_six, section_out, cotangent.transpose(1, 2, 0, 3), gain_six, bias_six, seg_half, counts,
        pick_large,
    )
    output = out_rows.transpose(2, 0, 1, 3)

    grad_six, par_six, st, *slots = call(
        back_six_kernel,
        (struct((px, wide), BF16), struct((8, wide)), st_mid, *mid_slots),
        place, to_batch(st), grad_final, xhat_six, inv_six, gain_six, seg_half, counts, e2_w, slope_five, xhat_five,
        flops=2 * matmul,
    )

    def own(xhat):
        return part(xhat, (None, *xhat.shape[1:]), (0,) * xhat.ndim)

    raws, st = swap_slots(slots), to_all(st)
    cols_five, par_five, st, *slots = call(
        back_spatial_kernel((1, 1), UNIT_TAPS, list(range(9)), s2_w[1], False),
        (struct((px, 9 * mid), BF16), struct((8, mid)), st_mid, *[struct((1, px, mid), BF16)] * nc),
        place, st, *raws, own(xhat_five), inv_five, params, seg_half, counts, source, slope_four[:, None],
        xhat_four[:, None], seg_half[None], *s2_w[0],
        flops=8 * matmul,
    )
    raws, st = swap_slots([x.reshape(px, mid) for x in slots]), to_all(st)
    (shares_two,) = call(
        grads_two_kernel, (struct((nb, e_cols + 9 * s_rows, mid), BF16),),
        place, grad_six, act_five, act_four, cols_five, flops=10 * matmul,
    )
    grad_four, par_four = call(
        back_plain_kernel((1, 0)),
        (struct((px, mid), BF16), struct((8, mid))),
        place, st, *raws, own(xhat_four), inv_four, params, seg_half, counts, after=[shares_two],
    )
    whole_grad_four, u_wide, st = call(
        back_section_kernel,
        (struct((nc, px, mid), BF16), struct((px, wide)), struct((nb, whole_tiles(3 * subs * wide_blocks), LANES))),
        place, *slots_of(grad_four), r2_w, grad_final, slope_section, xhat_three, xhat_short, seg_half,
        flops=2 * matmul,
    )

    grad_three, grad_short, par_wide, st, *slots = call(
        back_wide_kernel,
        (
            struct((px, wide), BF16),
            struct((px, wide), BF16),
            struct((8, wide)),
            st_mid,
            *mid_slots,
        ),
        place, to_batch(st), u_wide, xhat_three, xhat_short, inv_wide, first_wide_gain, seg_half, counts, e1_w,
        slope_two, xhat_two,
        flops=2 * matmul,
    )
    raws, st = swap_slots(slots), to_all(st)
    (shares_mixed,) = call(
        grads_mixed_kernel, (struct((nb, b_rows, mid), BF16),),
        place, section_low, whole_grad_four, grad_three, act_two, *shorts, grad_short, flops=8 * matmul,
    )
    owned_two, owned_mixed = to_owners(shares_two), to_owners(shares_mixed)
    half_one = struct((nb // 2, 9 * s_rows, mid), BF16)
    keep, send, par_two, st, *slots = call(
        back_spatial_kernel((0, 1), STRIDED_TAPS, STRIDED_ORDER, s1_w[1], True),
        (half_one, half_one, struct((8, mid)), st_mid, *[struct((4, px, mid), BF16)] * nc),
        place, st, *raws, own(xhat_two), inv_two, params, seg_half, counts, source, slope_one, xhat_one, seg_full,
        *s1_w[0], act_one,
        flops=16 * matmul, after=[shares_mixed, owned_two[0]],
    )
    raws, st = swap_slots(slots), to_all(st)
    send = lax.ppermute(send, "batch", [(i, i ^ 1) for i in range(nb)])
    (sum_one,) = call(total_kernel, (half_one,), place, keep, send)
    grad_one, par_one, *slots = call(
        back_one_kernel,
        (struct((4, px, mid), BF16), struct((8, mid)), *[struct((4, px, part_in), BF16)] * nc),
        place, st, *raws, own(xhat_one), inv_one, params, seg_full, counts, r1_w, grad_short, sc_w,
        flops=8 * matmul, after=[sum_one],
    )
    far_first, own_back = chan_swap(slots[3], 1), chan_swap(slots[1], 1)
    far_sum = (slots[2].astype(F32) + far_first.astype(F32)).astype(BF16)
    far_back = chan_swap(far_sum, 2)

    (shares,) = call(
        grads_reduce_kernel, (struct((nb, in_rows, mid), BF16),),
        place, *entries, grad_one, flops=4 * matmul, after=[far_sum, owned_mixed[0]],
    )
    turned, s2_own, sc_own = call(
        turn_kernel,
        (struct((turn_rows, mid), BF16), struct((9 * s_rows, mid)), struct((in_rows, wide))),
        place, *owned_two, *owned_mixed,
    )
    s1_total = lax.psum_scatter(
        sum_one, "batch", scatter_dimension=0, tiled=False,
        axis_index_groups=[list(range(first, nb, 2)) for first in range(2)],
    )
    e1_own, r2_own, e2_own, s1_total, r1_out = call(
        own_kernel,
        (
            struct((mid, e_cols)),
            struct((r2_rows, mid)),
            struct((mid, e_cols)),
            struct((9 * s_rows, mid)),
            struct((in_rows, mid)),
        ),
        place, turn_share(turned), s1_total, to_batch(shares),
    )
    mid_pair, wide_pair, wide_row = struct((2, mid)), struct((2, wide)), struct((1, wide))
    own_params_grad = call(
        param_kernel,
        (mid_pair, mid_pair, wide_pair, wide_pair, mid_pair, mid_pair, wide_row, wide_row),
        place, par_one, par_two, par_wide, par_four, par_five, par_six, after=[far_sum],
    )
    outs = (
        output,
        s1_total.reshape(3, 3, s_rows, mid),
        e1_own,
        sc_own,
        r2_own,
        s2_own.reshape(3, 3, s_rows, mid),
        e2_own,
        *own_params_grad[:-2],
        own_params_grad[-2][0],
        own_params_grad[-1][0],
    )
    (input_grad,) = call(
        input_kernel, (struct((side, side, crops, part_in)),), place, slots[0], own_back, far_back, seg_full,
        after=[own_params_grad[0]],
    )
    return outs[:1] + (input_grad.transpose(2, 0, 1, 3), r1_out) + outs[1:]


def solution(mesh):
    placed = (
        P("batch", None, None, "chan"),
        P("batch", "chan"),
        P(None, None, "batch", "chan"),
        P("chan", "batch"),
        P("batch", "chan"),
        P("batch", "chan"),
        P(None, None, "batch", "chan"),
        P("chan", "batch"),
        P(None, "chan"),
        P(None, "chan"),
        P(None, "chan"),
        P(None, "chan"),
        P(None, "chan"),
        P(None, "chan"),
        P("chan"),
        P("chan"),
        P(),
        P(),
        P(),
        P("batch", None, None, "chan"),
    )
    outs = (
        P("batch", None, None, "chan"),
        P("batch", None, None, "chan"),
        P("batch", "chan"),
        P(None, None, "batch", "chan"),
        P("chan", "batch"),
        P("batch", "chan"),
        P("batch", "chan"),
        P(None, None, "batch", "chan"),
        P("chan", "batch"),
        P(None, "chan"),
        P(None, "chan"),
        P(None, "chan"),
        P(None, "chan"),
        P(None, "chan"),
        P(None, "chan"),
        P("chan"),
        P("chan"),
    )
    return jax.shard_map(local, mesh=mesh, in_specs=placed, out_specs=outs, check_vma=False)
```

profile of v0, /device:TPU:4, one launch (start us, length us, event | category | flops | bytes accessed | tf_op | source)
XLA Modules:
  0.0 380.3 jit_solution(7192030251790310278)
XLA Ops:
  7.9 3.5 shard_map.368
  11.4 6.0 %all-to-all-start = ((bf16[8,256,128]{2,1,0:T(8,128)(2,1)}), bf16[8,256,128]{2,1,0:T(8,128)(2,1)}, u32[]{:S(2)}, u32[]{:S(2)}) async-start(bf16[8,256,128]{2,1,0:T(8,128)(2,1)} %get-tuple-element.126), calls=%async_computation | async-start | bytes 1048576 | tf_op jit(solution)/shard_map/all_to_all | solution.py:240
  17.4 4.7 %collective-permute-start.9 = (bf16[768,128]{1,0:T(8,128)(2,1)S(1)}, bf16[768,128]{1,0:T(8,128)(2,1)}, u32[]{:S(2)}, u32[]{:S(2)}) collective-permute-start(bf16[768,128]{1,0:T(8,128)(2,1)S(1)} %copy-done.12), channel_id=1, source_target_pairs={{0,0},{1,8},{2,16},{3,24},{4,4},{5,12},{6,20},{7,28},{8,1},{9,9},{... | collective-permute-start | bytes 589832 | tf_op jit(solution)/shard_map/ppermute | solution.py:252
  22.2 18.2 %collective-permute-done.9.refs_0_ = bf16[768,128]{1,0:T(8,128)(2,1)} collective-permute-done((bf16[768,128]{1,0:T(8,128)(2,1)S(1)}, bf16[768,128]{1,0:T(8,128)(2,1)}, u32[]{:S(2)}, u32[]{:S(2)}) %collective-permute-start.9) | collective-permute-done | bytes 196640 | tf_op jit(solution)/shard_map/ppermute | solution.py:252
  40.3 1.9 shard_map.372
  42.4 4.4 %all-to-all-start.1 = ((bf16[8,448,128]{2,1,0:T(8,128)(2,1)}), bf16[8,448,128]{2,1,0:T(8,128)(2,1)}, u32[]{:S(2)}, u32[]{:S(2)}) async-start(bf16[8,448,128]{2,1,0:T(8,128)(2,1)} %get-tuple-element.129), calls=%async_computation.1 | async-start | bytes 1835008 | tf_op jit(solution)/shard_map/all_to_all | solution.py:240
  52.6 3.7 shard_map.369
  56.3 2.0 collective-permute-start.2
  58.4 16.7 %all-to-all-done.1.refs_1_.refs_13_.refs_14_.refs_15_.refs_16_.refs_17_.refs_18_.refs_19_.refs_20_.refs_21_.refs_22_ = bf16[8,448,128]{2,1,0:T(8,128)(2,1)} async-done(((bf16[8,448,128]{2,1,0:T(8,128)(2,1)}), bf16[8,448,128]{2,1,0:T(8,128)(2,1)}, u32[]{:S(2)}, u32[]{:S(2)}) %all-to-all-start.1) | async-done | bytes 917536 | tf_op jit(solution)/shard_map/all_to_all | solution.py:240
  76.8 4.8 %all-to-all-start.2 = ((f32[32,8,128]{2,1,0:T(8,128)}), f32[32,8,128]{2,1,0:T(8,128)}, u32[]{:S(2)}, u32[]{:S(2)}) async-start(f32[32,8,128]{2,1,0:T(8,128)} %shard_map.370), calls=%async_computation.2 | async-start | bytes 262144 | tf_op jit(solution)/shard_map/all_to_all | solution.py:243
  83.0 2.8 collective-permute-done.5
  87.1 4.7 %all-to-all-done.2.refs_4_ = f32[32,8,128]{2,1,0:T(8,128)} async-done(((f32[32,8,128]{2,1,0:T(8,128)}), f32[32,8,128]{2,1,0:T(8,128)}, u32[]{:S(2)}, u32[]{:S(2)}) %all-to-all-start.2) | async-done | bytes 131104 | tf_op jit(solution)/shard_map/all_to_all | solution.py:243
  92.4 7.7 %shard_map.371 = (bf16[4,4,304,128]{3,2,1,0:T(8,128)(2,1)}, bf16[4,4,304,128]{3,2,1,0:T(8,128)(2,1)}, bf16[4,4,304,128]{3,2,1,0:T(8,128)(2,1)}, f32[8,128]{1,0:T...) custom-call(s32[2]{0:T(128)} %pad_add_fusion.p_ref, bf16[4,304,128]{2,1,0:T(8,128)(2,1)} %get-tuple-element.127.refs_0_, ...), custom_call_target="tpu_custom_call" | custom-call | flops 1593835520 | bytes 6609408 | tf_op jit(solution)/shard_map/pallas_call | solution.py:100
  100.2 3.9 %all-to-all-start.3 = ((f32[32,8,128]{2,1,0:T(8,128)}), f32[32,8,128]{2,1,0:T(8,128)}, u32[]{:S(2)}, u32[]{:S(2)}) async-start(f32[32,8,128]{2,1,0:T(8,128)} %get-tuple-element.131), calls=%async_computation.3 | async-start | bytes 262144 | tf_op jit(solution)/shard_map/all_to_all | solution.py:243
  106.0 2.9 shard_map.373.refs_10_.refs_2_
  109.5 2.2 collective-permute-done.7.refs_2_
  111.7 3.8 %shard_map.374 = (bf16[4,304,128]{2,1,0:T(8,128)(2,1)}, f32[4,304,128]{2,1,0:T(8,128)}, f32[4,304,128]{2,1,0:T(8,128)}, f32[8,128]{1,0:T(8,128)}, f32[304,512]{1,0:T(8,128)}, /*index=5*/f32[8,48,128]{2,1,0:T(8,128)}) custom-call(s32[2]{0:T(128)} %pad_add_fusion.p_ref, bf16[304,128]{1,0:T(8,128)(2,1)} %get-tuple-element.130.refs_0_, ...), custom_call_target="tpu_custom_call" | custom-call | flops 318767104 | bytes 4015616 | tf_op jit(solution)/shard_map/pallas_call | solution.py:100
  115.6 14.1 %all_to_all.75.refs_0_ = f32[8,48,128]{2,1,0:T(8,128)} all-to-all(f32[8,48,128]{2,1,0:T(8,128)} %get-tuple-element.136), channel_id=1, replica_groups=mesh['batch'=8,'chan'=4] {'batch'}, dimensions={0} | all-to-all | bytes 393216 | tf_op jit(solution)/shard_map/all_to_all | solution.py:240
  129.6 4.2 %shard_map.375 = (f32[304,512]{1,0:T(8,128)}, f32[304,512]{1,0:T(8,128)}, f32[304,512]{1,0:T(8,128)}, f32[304,512]{1,0:T(8,128)}, f32[8,512]{1,0:T(8,128)}, /*in...) custom-call(s32[2]{0:T(128)} %pad_add_fusion.p_ref, ...), custom_call_target="tpu_custom_call" | custom-call | flops 318767104 | bytes 5117440 | tf_op jit(solution)/shard_map/pallas_call | solution.py:100
  135.7 3.7 collective-permute-done.11.refs_2_
  140.1 2.0 shard_map.376
  142.1 4.1 %all-to-all-start.5 = ((f32[32,8,128]{2,1,0:T(8,128)}), f32[32,8,128]{2,1,0:T(8,128)}, u32[]{:S(2)}, u32[]{:S(2)}) async-start(f32[32,8,128]{2,1,0:T(8,128)} %get-tuple-element.143), calls=%async_computation.5 | async-start | bytes 262144 | tf_op jit(solution)/shard_map/all_to_all | solution.py:243
  148.1 7.4 %all-gather.11.cloned.1.call-done = bf16[6656,128]{1,0:T(8,128)(2,1)} async-done(((bf16[832,128]{1,0:T(8,128)(2,1)}), bf16[6656,128]{1,0:T(8,128)(2,1)}) %all-gather.11.cloned.1.call-update) | async-done | bytes 1703952 | tf_op jit(solution)/shard_map/all_gather | solution.py:282
  155.5 5.3 %shard_map.377 = (bf16[4,304,128]{2,1,0:T(8,128)(2,1)}, f32[4,304,128]{2,1,0:T(8,128)}, f32[4,304,128]{2,1,0:T(8,128)}, f32[8,128]{1,0:T(8,128)}, bf16[304,128]{1,0:T(8,128)(2,1)}, /*index=5*/f32[32,8,128]{2,1,0:T(8,128)}) custom-call(s32[2]{0:T(128)} %pad_add_fusion.p_ref, bf16[304,128]{1,0:T(8,128)(2,1)} %get-tuple-element.142.refs_0_, ...), custom_call_target="tpu_custom_call" | custom-call | flops 1275068416 | bytes 3457536 | tf_op jit(solution)/shard_map/pallas_call | solution.py:100
  160.8 3.7 all-to-all-start.6
  166.5 3.5 collective-permute-done.18.refs_3_
  170.0 2.2 collective-permute-done.17.refs_2_
  172.2 3.5 shard_map.378
  175.7 12.1 %all_to_all.76.refs_0_ = f32[8,24,128]{2,1,0:T(8,128)} all-to-all(f32[8,24,128]{2,1,0:T(8,128)} %get-tuple-element.147), channel_id=1, replica_groups=mesh['batch'=8,'chan'=4] {'batch'}, dimensions={0} | all-to-all | bytes 196608 | tf_op jit(solution)/shard_map/all_to_all | solution.py:240
  187.8 4.4 %shard_map.379 = (f32[7,7,16,512]{3,2,1,0:T(8,128)}, f32[304,512]{1,0:T(8,128)}, f32[304,512]{1,0:T(8,128)}, f32[8,512]{1,0:T(8,128)}, f32[8,24,128]{2,1,0:T(8,128)}) custom-call(s32[2]{0:T(128)} %pad_add_fusion.p_ref, f32[8,24,128]{2,1,0:T(8,128)} %all_to_all.76.refs_0_, f32[304,512]{1,0:T(8,128)} %get-tuple-element.148.refs_1_, ...), custom_call_target="tpu_custom_call" | custom-call | flops 100000000 | bytes 5137920 | tf_op jit(solution)/shard_map/pallas_call | solution.py:100
  192.2 11.1 %all_to_all.77.refs_0_ = f32[8,24,128]{2,1,0:T(8,128)} all-to-all(f32[8,24,128]{2,1,0:T(8,128)} %get-tuple-element.151), channel_id=1, replica_groups=mesh['batch'=8,'chan'=4] {'batch'}, dimensions={0} | all-to-all | bytes 196608 | tf_op jit(solution)/shard_map/all_to_all | solution.py:240
  203.3 3.6 shard_map.380
  206.9 3.9 %all-to-all-start.9 = ((f32[32,8,128]{2,1,0:T(8,128)}), f32[32,8,128]{2,1,0:T(8,128)}, u32[]{:S(2)}, u32[]{:S(2)}) async-start(f32[32,8,128]{2,1,0:T(8,128)} %get-tuple-element.157), calls=%async_computation.9 | async-start | bytes 262144 | tf_op jit(solution)/shard_map/all_to_all | solution.py:243
  212.7 4.4 %collective-permute-done.20.refs_3_ = bf16[304,128]{1,0:T(8,128)(2,1)} collective-permute-done((bf16[304,128]{1,0:T(8,128)(2,1)}, bf16[304,128]{1,0:T(8,128)(2,1)}, u32[]{:S(2)}, u32[]{:S(2)}) %collective-permute-start.20) | collective-permute-done | bytes 77856 | tf_op jit(solution)/shard_map/ppermute | solution.py:231
  218.1 5.7 %shard_map.381 = (bf16[304,1152]{1,0:T(8,128)(2,1)}, f32[8,128]{1,0:T(8,128)}, f32[32,8,128]{2,1,0:T(8,128)}, bf16[1,304,128]{2,1,0:T(8,128)(2,1)}, bf16[1,304,1...) custom-call(s32[2]{0:T(128)} %pad_add_fusion.p_ref, ...), custom_call_target="tpu_custom_call" | custom-call | flops 1275068416 | bytes 4233216 | tf_op jit(solution)/shard_map/pallas_call | solution.py:100
  223.8 3.9 %shard_map.382.refs_10_ = bf16[8,832,128]{2,1,0:T(8,128)(2,1)} custom-call(s32[2]{0:T(128)} %pad_add_fusion.p_ref, bf16[304,512]{1,0:T(8,128)(2,1)} %get-tuple-element.171.refs_0_, bf16[4,304,128]{2,1,0:T(8,128)(2,1)} %get-tuple-element.172.refs_1_, bf16[4,304,128]{2,1,0:T(8,128)(2,1)} %get-tuple-element.173.refs_2_, ...), custom_call_target="tpu_custom_call" | custom-call | flops 1593835520 | bytes 3338240 | tf_op jit(solution)/shard_map/pallas_call | solution.py:100
  227.7 5.3 %all-to-all-start.10 = ((f32[32,8,128]{2,1,0:T(8,128)}), f32[32,8,128]{2,1,0:T(8,128)}, u32[]{:S(2)}, u32[]{:S(2)}) async-start(f32[32,8,128]{2,1,0:T(8,128)} %get-tuple-element.165), calls=%async_computation.10 | async-start | bytes 262144 | tf_op jit(solution)/shard_map/all_to_all | solution.py:243
  233.1 9.5 %reduce-scatter.6.cloned.1.call-start = ((), (), s32[]{:S(2)}) async-start(), calls=%async_computation.19 | async-start | bytes 2621440 | tf_op jit(solution)/shard_map/reduce_scatter | solution.py:910
  244.5 3.6 collective-permute-done.23.refs_3_
  248.6 2.1 shard_map.383
  253.1 1.8 collective-permute-done.27.refs_3_
  254.9 2.5 collective-permute-done.26.refs_2_
  257.4 3.6 shard_map.384
  261.0 13.2 %all_to_all.78.refs_0_ = f32[8,40,128]{2,1,0:T(8,128)} all-to-all(f32[8,40,128]{2,1,0:T(8,128)} %get-tuple-element.179), channel_id=1, replica_groups=mesh['batch'=8,'chan'=4] {'batch'}, dimensions={0} | all-to-all | bytes 327680 | tf_op jit(solution)/shard_map/all_to_all | solution.py:240
  274.2 4.1 %shard_map.385 = (bf16[304,512]{1,0:T(8,128)(2,1)}, bf16[304,512]{1,0:T(8,128)(2,1)}, f32[8,512]{1,0:T(8,128)}, f32[32,8,128]{2,1,0:T(8,128)}, bf16[304,128]{1,0...) custom-call(s32[2]{0:T(128)} %pad_add_fusion.p_ref, ...), custom_call_target="tpu_custom_call" | custom-call | flops 318767104 | bytes 4916736 | tf_op jit(solution)/shard_map/pallas_call | solution.py:100
  278.3 4.5 %shard_map.386.refs_24_ = bf16[8,1024,128]{2,1,0:T(8,128)(2,1)} custom-call(s32[2]{0:T(128)} %pad_add_fusion.p_ref, bf16[304,512]{1,0:T(8,128)(2,1)} %get-tuple-element.193.refs_0_, bf16[4,304,128]{2,1,0:T(8,128)(2,1)} %get-tuple-element.194.refs_1_, bf16[304,512]{1,0:T(8,128)(2,1)} %get-tuple-element.195.refs_2_, ...), custom_call_target="tpu_custom_call" | custom-call | flops 1275068416 | bytes 4276224 | tf_op jit(solution)/shard_map/pallas_call | solution.py:100
  282.8 4.0 %all-to-all-start.12 = ((f32[32,8,128]{2,1,0:T(8,128)}), f32[32,8,128]{2,1,0:T(8,128)}, u32[]{:S(2)}, u32[]{:S(2)}) async-start(f32[32,8,128]{2,1,0:T(8,128)} %get-tuple-element.184), calls=%async_computation.12 | async-start | bytes 262144 | tf_op jit(solution)/shard_map/all_to_all | solution.py:243
  288.7 4.0 %collective-permute-done.29.refs_3_ = bf16[304,128]{1,0:T(8,128)(2,1)} collective-permute-done((bf16[304,128]{1,0:T(8,128)(2,1)S(1)}, bf16[304,128]{1,0:T(8,128)(2,1)}, u32[]{:S(2)}, u32[]{:S(2)}) %collective-permute-start.29) | collective-permute-done | bytes 77856 | tf_op jit(solution)/shard_map/ppermute | solution.py:231
  293.7 3.7 all-to-all-done.12.refs_0_
  297.3 7.0 %shard_map.387 = (bf16[4,576,128]{2,1,0:T(8,128)(2,1)}, bf16[4,576,128]{2,1,0:T(8,128)(2,1)}, f32[8,128]{1,0:T(8,128)}, f32[32,8,128]{2,1,0:T(8,128)}, bf16[4,30...) custom-call(s32[2]{0:T(128)} %pad_add_fusion.p_ref, ...), custom_call_target="tpu_custom_call" | custom-call | flops 2550136832 | bytes 8165888 | tf_op jit(solution)/shard_map/pallas_call | solution.py:100
  307.7 3.4 all-to-all-start.13
  311.2 9.4 %collective-permute-done.34.refs_1_ = bf16[4,576,128]{2,1,0:T(8,128)(2,1)} collective-permute-done((bf16[4,576,128]{2,1,0:T(8,128)(2,1)}, bf16[4,576,128]{2,1,0:T(8,128)(2,1)}, u32[]{:S(2)}, u32[]{:S(2)}) %collective-permute-start.34) | collective-permute-done | bytes 589856 | tf_op jit(solution)/shard_map/ppermute | solution.py:1053
  320.6 2.2 shard_map.388.refs_13_
  324.0 5.1 %shard_map.389 = (bf16[4,304,128]{2,1,0:T(8,128)(2,1)}, f32[8,128]{1,0:T(8,128)}, bf16[4,304,256]{2,1,0:T(8,128)(2,1)}, bf16[4,304,256]{2,1,0:T(8,128)(2,1)}, bf...) custom-call(s32[2]{0:T(128)} %pad_add_fusion.p_ref, f32[32,8,128]{2,1,0:T(8,128)} %all-to-all-done.13.refs_0_, ...), custom_call_target="tpu_custom_call" | custom-call | flops 1275068416 | bytes 6178816 | tf_op jit(solution)/shard_map/pallas_call | solution.py:100
  331.4 2.1 add_convert_fusion.refs_6_.refs_5_
  336.4 3.5 shard_map.393
  339.9 4.0 %all-to-all-start.14 = ((bf16[8,128,128]{2,1,0:T(8,128)(2,1)}), bf16[8,128,128]{2,1,0:T(8,128)(2,1)}, u32[]{:S(2)}, u32[]{:S(2)}) async-start(bf16[8,128,128]{2,1,0:T(8,128)(2,1)} %shard_map.393), calls=%async_computation.17 | async-start | bytes 524288 | tf_op jit(solution)/shard_map/all_to_all | solution.py:240
  344.9 2.0 collective-permute-start.38
  346.8 7.1 %collective-permute-done.38.refs_1_ = bf16[832,128]{1,0:T(8,128)(2,1)} collective-permute-done((bf16[832,128]{1,0:T(8,128)(2,1)S(1)}, bf16[832,128]{1,0:T(8,128)(2,1)}, u32[]{:S(2)}, u32[]{:S(2)}) %collective-permute-start.38) | collective-permute-done | bytes 213024 | tf_op jit(solution)/shard_map/ppermute | solution.py:914
  353.9 2.3 shard_map.392
  356.2 5.3 %collective-permute-start.40 = (bf16[768,128]{1,0:T(8,128)(2,1)}, bf16[768,128]{1,0:T(8,128)(2,1)}, u32[]{:S(2)}, u32[]{:S(2)}) collective-permute-start(bf16[768,128]{1,0:T(8,128)(2,1)} %get-tuple-element.217), channel_id=1, source_target_pairs={{0,0},{1,8},{2,16},{3,24},{4,4},{5,12},{6,20},{7,28},{8,1},{9,9},{... | collective-permute-start | bytes 589832 | tf_op jit(solution)/shard_map/ppermute | solution.py:252
  362.9 3.9 %shard_map.391 = f32[14,14,16,256]{3,2,1,0:T(8,128)} custom-call(s32[2]{0:T(128)} %pad_add_fusion.p_ref, bf16[4,304,256]{2,1,0:T(8,128)(2,1)} %get-tuple-element.206.refs_0_, bf16[4,304,256]{2,1,0:T(8,128)(2,1)} %collective-permute-done.35.refs_1_, bf16[4,304,256]{2,1,0:T(8,128)(2,1)} %collective-permute-done.37.refs_2_, ...), custom_call_target="tpu_custom_call" | custom-call | flops 100000000 | bytes 5117952 | tf_op jit(solution)/shard_map/pallas_call | solution.py:100
  366.8 4.5 %collective-permute-done.40.refs_0_ = bf16[768,128]{1,0:T(8,128)(2,1)} collective-permute-done((bf16[768,128]{1,0:T(8,128)(2,1)}, bf16[768,128]{1,0:T(8,128)(2,1)}, u32[]{:S(2)}, u32[]{:S(2)}) %collective-permute-start.40) | collective-permute-done | bytes 196640 | tf_op jit(solution)/shard_map/ppermute | solution.py:252
  371.3 2.0 shard_map.394
  (153 shorter events, 43.4 us)
Async XLA Ops:
  7.2 45.4 %all-gather.7.cloned.1.call-start = ((), (), s32[]{:S(2)}) async-start(), calls=%async_computation.21 | async-start | bytes 3112960 | tf_op jit(solution)/shard_map/all_gather | solution.py:300
  11.4 28.9 %all-to-all-start = ((bf16[8,256,128]{2,1,0:T(8,128)(2,1)}), bf16[8,256,128]{2,1,0:T(8,128)(2,1)}, u32[]{:S(2)}, u32[]{:S(2)}) async-start(bf16[8,256,128]{2,1,0:T(8,128)(2,1)} %get-tuple-element.126), calls=%async_computation | async-start | bytes 1048576 | tf_op jit(solution)/shard_map/all_to_all | solution.py:240
  17.4 88.7 %all-gather.9.cloned.1.call-start = ((), (), s32[]{:S(2)}) async-start(), calls=%async_computation.22 | async-start | bytes 2359296 | tf_op jit(solution)/shard_map/all_gather | solution.py:282
  17.4 22.9 %collective-permute-start.9 = (bf16[768,128]{1,0:T(8,128)(2,1)S(1)}, bf16[768,128]{1,0:T(8,128)(2,1)}, u32[]{:S(2)}, u32[]{:S(2)}) collective-permute-start(bf16[768,128]{1,0:T(8,128)(2,1)S(1)} %copy-done.12), channel_id=1, source_target_pairs={{0,0},{1,8},{2,16},{3,24},{4,4},{5,12},{6,20},{7,28},{8,1},{9,9},{... | collective-permute-start | bytes 589832 | tf_op jit(solution)/shard_map/ppermute | solution.py:252
  42.3 6.2 %copy-start.1 = (s32[304,1]{0,1:T(1,128)S(1)}, s32[304,1]{0,1:T(1,128)}, u32[]{:S(2)}) copy-start(s32[304,1]{0,1:T(1,128)} %constant.94) | copy-start | bytes 3652
  42.3 6.2 %copy-start.2 = (s32[304,1]{0,1:T(1,128)S(1)}, s32[304,1]{0,1:T(1,128)}, u32[]{:S(2)}) copy-start(s32[304,1]{0,1:T(1,128)} %constant.93) | copy-start | bytes 3652
  42.3 6.2 %copy-start.3 = (s32[304,1]{0,1:T(1,128)S(1)}, s32[304,1]{0,1:T(1,128)}, u32[]{:S(2)}) copy-start(s32[304,1]{0,1:T(1,128)} %constant.92) | copy-start | bytes 3652
  42.4 32.8 %all-to-all-start.1 = ((bf16[8,448,128]{2,1,0:T(8,128)(2,1)}), bf16[8,448,128]{2,1,0:T(8,128)(2,1)}, u32[]{:S(2)}, u32[]{:S(2)}) async-start(bf16[8,448,128]{2,1,0:T(8,128)(2,1)} %get-tuple-element.129), calls=%async_computation.1 | async-start | bytes 1835008 | tf_op jit(solution)/shard_map/all_to_all | solution.py:240
  46.7 108.7 %all-gather.11.cloned.1.call-start = ((), (), s32[]{:S(2)}) async-start(), calls=%async_computation.23 | async-start | bytes 1916928 | tf_op jit(solution)/shard_map/all_gather | solution.py:282
  48.1 34.3 %collective-permute-start.4 = (f32[8,128]{1,0:T(8,128)}, f32[8,128]{1,0:T(8,128)}, u32[]{:S(2)}, u32[]{:S(2)}) collective-permute-start(f32[8,128]{1,0:T(8,128)} %get-tuple-element.244), channel_id=1, source_target_pairs={{0,2},{1,3},{2,0},{3,1},{4,6},{5,7},{6,4},{7,5},{8,10},{9,11},{10,... | collective-permute-start | bytes 12296 | tf_op jit(solution)/shard_map/ppermute | solution.py:231
  48.1 34.9 %collective-permute-start.3 = (f32[8,128]{1,0:T(8,128)}, f32[8,128]{1,0:T(8,128)}, u32[]{:S(2)}, u32[]{:S(2)}) collective-permute-start(f32[8,128]{1,0:T(8,128)} %get-tuple-element.244), channel_id=1, source_target_pairs={{0,1},{1,0},{2,3},{3,2},{4,5},{5,4},{6,7},{7,6},{8,9},{9,8},{10,11... | collective-permute-start | bytes 12296 | tf_op jit(solution)/shard_map/ppermute | solution.py:231
  56.3 35.4 %collective-permute-start.2 = (bf16[4,304,128]{2,1,0:T(8,128)(2,1)}, bf16[4,304,128]{2,1,0:T(8,128)(2,1)}, u32[]{:S(2)}, u32[]{:S(2)}) collective-permute-start(bf16[4,304,128]{2,1,0:T(8,128)(2,1)} %get-tuple-element.127.refs_0_), channel_id=1, source_target_pairs={{0,3},{1,2},{2,1},{3,0},{4,7},{5,6},{6,5},{7,4},{8,11},{9,10},{10,... | collective-permute-start | bytes 933896 | tf_op jit(solution)/shard_map/ppermute | solution.py:231
  58.3 33.5 %collective-permute-start.1 = (bf16[4,304,128]{2,1,0:T(8,128)(2,1)}, bf16[4,304,128]{2,1,0:T(8,128)(2,1)}, u32[]{:S(2)}, u32[]{:S(2)}) collective-permute-start(bf16[4,304,128]{2,1,0:T(8,128)(2,1)} %get-tuple-element.127.refs_0_), channel_id=1, source_target_pairs={{0,2},{1,3},{2,0},{3,1},{4,6},{5,7},{6,4},{7,5},{8,10},{9,11},{10,... | collective-permute-start | bytes 933896 | tf_op jit(solution)/shard_map/ppermute | solution.py:231
  58.4 33.4 %collective-permute-start = (bf16[4,304,128]{2,1,0:T(8,128)(2,1)}, bf16[4,304,128]{2,1,0:T(8,128)(2,1)}, u32[]{:S(2)}, u32[]{:S(2)}) collective-permute-start(bf16[4,304,128]{2,1,0:T(8,128)(2,1)} %get-tuple-element.127.refs_0_), channel_id=1, source_target_pairs={{0,1},{1,0},{2,3},{3,2},{4,5},{5,4},{6,7},{7,6},{8,9},{9,8},{10,11... | collective-permute-start | bytes 933896 | tf_op jit(solution)/shard_map/ppermute | solution.py:231
  76.8 15.0 %all-to-all-start.2 = ((f32[32,8,128]{2,1,0:T(8,128)}), f32[32,8,128]{2,1,0:T(8,128)}, u32[]{:S(2)}, u32[]{:S(2)}) async-start(f32[32,8,128]{2,1,0:T(8,128)} %shard_map.370), calls=%async_computation.2 | async-start | bytes 262144 | tf_op jit(solution)/shard_map/all_to_all | solution.py:243
  82.5 3.3 collective-permute-start.5
  100.2 11.6 %all-to-all-start.3 = ((f32[32,8,128]{2,1,0:T(8,128)}), f32[32,8,128]{2,1,0:T(8,128)}, u32[]{:S(2)}, u32[]{:S(2)}) async-start(f32[32,8,128]{2,1,0:T(8,128)} %get-tuple-element.131), calls=%async_computation.3 | async-start | bytes 262144 | tf_op jit(solution)/shard_map/all_to_all | solution.py:243
  104.1 5.4 %collective-permute-start.8 = (bf16[304,128]{1,0:T(8,128)(2,1)}, bf16[304,128]{1,0:T(8,128)(2,1)}, u32[]{:S(2)}, u32[]{:S(2)}) collective-permute-start(bf16[304,128]{1,0:T(8,128)(2,1)} %get-tuple-element.130.refs_0_), channel_id=1, source_target_pairs={{0,3},{1,2},{2,1},{3,0},{4,7},{5,6},{6,5},{7,4},{8,11},{9,10},{10,... | collective-permute-start | bytes 233480 | tf_op jit(solution)/shard_map/ppermute | solution.py:231
  104.3 7.4 %collective-permute-start.7 = (bf16[304,128]{1,0:T(8,128)(2,1)}, bf16[304,128]{1,0:T(8,128)(2,1)}, u32[]{:S(2)}, u32[]{:S(2)}) collective-permute-start(bf16[304,128]{1,0:T(8,128)(2,1)} %get-tuple-element.130.refs_0_), channel_id=1, source_target_pairs={{0,2},{1,3},{2,0},{3,1},{4,6},{5,7},{6,4},{7,5},{8,10},{9,11},{10,... | collective-permute-start | bytes 233480 | tf_op jit(solution)/shard_map/ppermute | solution.py:231
  106.0 5.8 %collective-permute-start.6 = (bf16[304,128]{1,0:T(8,128)(2,1)}, bf16[304,128]{1,0:T(8,128)(2,1)}, u32[]{:S(2)}, u32[]{:S(2)}) collective-permute-start(bf16[304,128]{1,0:T(8,128)(2,1)} %get-tuple-element.130.refs_0_), channel_id=1, source_target_pairs={{0,1},{1,0},{2,3},{3,2},{4,5},{5,4},{6,7},{7,6},{8,9},{9,8},{10,11... | collective-permute-start | bytes 233480 | tf_op jit(solution)/shard_map/ppermute | solution.py:231
  133.8 1.9 collective-permute-start.10
  133.8 5.5 %collective-permute-start.11 = (bf16[304,128]{1,0:T(8,128)(2,1)}, bf16[304,128]{1,0:T(8,128)(2,1)}, u32[]{:S(2)}, u32[]{:S(2)}) collective-permute-start(bf16[304,128]{1,0:T(8,128)(2,1)} %get-tuple-element.140), channel_id=1, source_target_pairs={{0,2},{1,3},{2,0},{3,1},{4,6},{5,7},{6,4},{7,5},{8,10},{9,11},{10,... | collective-permute-start | bytes 233480 | tf_op jit(solution)/shard_map/ppermute | solution.py:231
  134.7 5.5 %collective-permute-start.12 = (bf16[304,128]{1,0:T(8,128)(2,1)}, bf16[304,128]{1,0:T(8,128)(2,1)}, u32[]{:S(2)}, u32[]{:S(2)}) collective-permute-start(bf16[304,128]{1,0:T(8,128)(2,1)} %get-tuple-element.141), channel_id=1, source_target_pairs={{0,3},{1,2},{2,1},{3,0},{4,7},{5,6},{6,5},{7,4},{8,11},{9,10},{10,... | collective-permute-start | bytes 233480 | tf_op jit(solution)/shard_map/ppermute | solution.py:231
  142.1 13.4 %all-to-all-start.5 = ((f32[32,8,128]{2,1,0:T(8,128)}), f32[32,8,128]{2,1,0:T(8,128)}, u32[]{:S(2)}, u32[]{:S(2)}) async-start(f32[32,8,128]{2,1,0:T(8,128)} %get-tuple-element.143), calls=%async_computation.5 | async-start | bytes 262144 | tf_op jit(solution)/shard_map/all_to_all | solution.py:243
  146.2 9.3 %collective-permute-start.15 = (bf16[304,128]{1,0:T(8,128)(2,1)}, bf16[304,128]{1,0:T(8,128)(2,1)}, u32[]{:S(2)}, u32[]{:S(2)}) collective-permute-start(bf16[304,128]{1,0:T(8,128)(2,1)} %get-tuple-element.142.refs_0_), channel_id=1, source_target_pairs={{0,3},{1,2},{2,1},{3,0},{4,7},{5,6},{6,5},{7,4},{8,11},{9,10},{10,... | collective-permute-start | bytes 233480 | tf_op jit(solution)/shard_map/ppermute | solution.py:231
  146.4 9.1 %collective-permute-start.14 = (bf16[304,128]{1,0:T(8,128)(2,1)}, bf16[304,128]{1,0:T(8,128)(2,1)}, u32[]{:S(2)}, u32[]{:S(2)}) collective-permute-start(bf16[304,128]{1,0:T(8,128)(2,1)} %get-tuple-element.142.refs_0_), channel_id=1, source_target_pairs={{0,2},{1,3},{2,0},{3,1},{4,6},{5,7},{6,4},{7,5},{8,10},{9,11},{10,... | collective-permute-start | bytes 233480 | tf_op jit(solution)/shard_map/ppermute | solution.py:231
  148.0 7.4 %collective-permute-start.13 = (bf16[304,128]{1,0:T(8,128)(2,1)}, bf16[304,128]{1,0:T(8,128)(2,1)}, u32[]{:S(2)}, u32[]{:S(2)}) collective-permute-start(bf16[304,128]{1,0:T(8,128)(2,1)} %get-tuple-element.142.refs_0_), channel_id=1, source_target_pairs={{0,1},{1,0},{2,3},{3,2},{4,5},{5,4},{6,7},{7,6},{8,9},{9,8},{10,11... | collective-permute-start | bytes 233480 | tf_op jit(solution)/shard_map/ppermute | solution.py:231
  160.8 11.4 %all-to-all-start.6 = ((f32[32,8,128]{2,1,0:T(8,128)}), f32[32,8,128]{2,1,0:T(8,128)}, u32[]{:S(2)}, u32[]{:S(2)}) async-start(f32[32,8,128]{2,1,0:T(8,128)} %get-tuple-element.146), calls=%async_computation.6 | async-start | bytes 262144 | tf_op jit(solution)/shard_map/all_to_all | solution.py:243
  164.5 5.4 %collective-permute-start.18 = (bf16[304,128]{1,0:T(8,128)(2,1)}, bf16[304,128]{1,0:T(8,128)(2,1)}, u32[]{:S(2)}, u32[]{:S(2)}) collective-permute-start(bf16[304,128]{1,0:T(8,128)(2,1)} %get-tuple-element.145.refs_0_), channel_id=1, source_target_pairs={{0,3},{1,2},{2,1},{3,0},{4,7},{5,6},{6,5},{7,4},{8,11},{9,10},{10,... | collective-permute-start | bytes 233480 | tf_op jit(solution)/shard_map/ppermute | solution.py:231
  164.7 7.4 %collective-permute-start.17 = (bf16[304,128]{1,0:T(8,128)(2,1)}, bf16[304,128]{1,0:T(8,128)(2,1)}, u32[]{:S(2)}, u32[]{:S(2)}) collective-permute-start(bf16[304,128]{1,0:T(8,128)(2,1)} %get-tuple-element.145.refs_0_), channel_id=1, source_target_pairs={{0,2},{1,3},{2,0},{3,1},{4,6},{5,7},{6,4},{7,5},{8,10},{9,11},{10,... | collective-permute-start | bytes 233480 | tf_op jit(solution)/shard_map/ppermute | solution.py:231
  166.4 5.8 %collective-permute-start.16 = (bf16[304,128]{1,0:T(8,128)(2,1)}, bf16[304,128]{1,0:T(8,128)(2,1)}, u32[]{:S(2)}, u32[]{:S(2)}) collective-permute-start(bf16[304,128]{1,0:T(8,128)(2,1)} %get-tuple-element.145.refs_0_), channel_id=1, source_target_pairs={{0,1},{1,0},{2,3},{3,2},{4,5},{5,4},{6,7},{7,6},{8,9},{9,8},{10,11... | collective-permute-start | bytes 233480 | tf_op jit(solution)/shard_map/ppermute | solution.py:231
  206.9 11.2 %all-to-all-start.9 = ((f32[32,8,128]{2,1,0:T(8,128)}), f32[32,8,128]{2,1,0:T(8,128)}, u32[]{:S(2)}, u32[]{:S(2)}) async-start(f32[32,8,128]{2,1,0:T(8,128)} %get-tuple-element.157), calls=%async_computation.9 | async-start | bytes 262144 | tf_op jit(solution)/shard_map/all_to_all | solution.py:243
  210.7 86.6 %reduce-scatter.4.cloned.1.call-start = ((), (), s32[]{:S(2)}) async-start(), calls=%async_computation.18 | async-start | bytes 2129920 | tf_op jit(solution)/shard_map/reduce_scatter | solution.py:910
  210.8 1.9 collective-permute-start.19
  211.0 6.1 %collective-permute-start.20 = (bf16[304,128]{1,0:T(8,128)(2,1)}, bf16[304,128]{1,0:T(8,128)(2,1)}, u32[]{:S(2)}, u32[]{:S(2)}) collective-permute-start(bf16[304,128]{1,0:T(8,128)(2,1)} %get-tuple-element.160), channel_id=1, source_target_pairs={{0,2},{1,3},{2,0},{3,1},{4,6},{5,7},{6,4},{7,5},{8,10},{9,11},{10,... | collective-permute-start | bytes 233480 | tf_op jit(solution)/shard_map/ppermute | solution.py:231
  211.4 6.7 %collective-permute-start.21 = (bf16[304,128]{1,0:T(8,128)(2,1)}, bf16[304,128]{1,0:T(8,128)(2,1)}, u32[]{:S(2)}, u32[]{:S(2)}) collective-permute-start(bf16[304,128]{1,0:T(8,128)(2,1)} %get-tuple-element.161), channel_id=1, source_target_pairs={{0,3},{1,2},{2,1},{3,0},{4,7},{5,6},{6,5},{7,4},{8,11},{9,10},{10,... | collective-permute-start | bytes 233480 | tf_op jit(solution)/shard_map/ppermute | solution.py:231
  227.7 14.9 %copy-start.16 = (bf16[1,304,128]{2,1,0:T(8,128)(2,1)S(1)}, bf16[1,304,128]{2,1,0:T(8,128)(2,1)}, u32[]{:S(2)}) copy-start(bf16[1,304,128]{2,1,0:T(8,128)(2,1)} %get-tuple-element.167) | copy-start | bytes 233476
  227.7 15.1 %copy-start.14 = (bf16[1,304,128]{2,1,0:T(8,128)(2,1)S(1)}, bf16[1,304,128]{2,1,0:T(8,128)(2,1)}, u32[]{:S(2)}) copy-start(bf16[1,304,128]{2,1,0:T(8,128)(2,1)} %get-tuple-element.168) | copy-start | bytes 233476
  227.7 15.5 %copy-start.13 = (bf16[1,304,128]{2,1,0:T(8,128)(2,1)S(1)}, bf16[1,304,128]{2,1,0:T(8,128)(2,1)}, u32[]{:S(2)}) copy-start(bf16[1,304,128]{2,1,0:T(8,128)(2,1)} %get-tuple-element.169) | copy-start | bytes 233476
  227.7 20.9 %all-to-all-start.10 = ((f32[32,8,128]{2,1,0:T(8,128)}), f32[32,8,128]{2,1,0:T(8,128)}, u32[]{:S(2)}, u32[]{:S(2)}) async-start(f32[32,8,128]{2,1,0:T(8,128)} %get-tuple-element.165), calls=%async_computation.10 | async-start | bytes 262144 | tf_op jit(solution)/shard_map/all_to_all | solution.py:243
  233.1 100.9 %reduce-scatter.6.cloned.1.call-start = ((), (), s32[]{:S(2)}) async-start(), calls=%async_computation.19 | async-start | bytes 2621440 | tf_op jit(solution)/shard_map/reduce_scatter | solution.py:910
  242.6 1.9 collective-permute-start.22
  242.8 5.3 %collective-permute-start.23 = (bf16[304,128]{1,0:T(8,128)(2,1)S(1)}, bf16[304,128]{1,0:T(8,128)(2,1)}, u32[]{:S(2)}, u32[]{:S(2)}) collective-permute-start(bf16[304,128]{1,0:T(8,128)(2,1)S(1)} %bitcast.106), channel_id=1, source_target_pairs={{0,2},{1,3},{2,0},{3,1},{4,6},{5,7},{6,4},{7,5},{8,10},{9,11},{10,... | collective-permute-start | bytes 233480 | tf_op jit(solution)/shard_map/ppermute | solution.py:231
  243.2 5.5 %collective-permute-start.24 = (bf16[304,128]{1,0:T(8,128)(2,1)S(1)}, bf16[304,128]{1,0:T(8,128)(2,1)}, u32[]{:S(2)}, u32[]{:S(2)}) collective-permute-start(bf16[304,128]{1,0:T(8,128)(2,1)S(1)} %bitcast.105), channel_id=1, source_target_pairs={{0,3},{1,2},{2,1},{3,0},{4,7},{5,6},{6,5},{7,4},{8,11},{9,10},{10,... | collective-permute-start | bytes 233480 | tf_op jit(solution)/shard_map/ppermute | solution.py:231
  250.8 4.1 %collective-permute-start.27 = (bf16[304,128]{1,0:T(8,128)(2,1)}, bf16[304,128]{1,0:T(8,128)(2,1)}, u32[]{:S(2)}, u32[]{:S(2)}) collective-permute-start(bf16[304,128]{1,0:T(8,128)(2,1)} %get-tuple-element.175.refs_0_), channel_id=1, source_target_pairs={{0,3},{1,2},{2,1},{3,0},{4,7},{5,6},{6,5},{7,4},{8,11},{9,10},{10,... | collective-permute-start | bytes 233480 | tf_op jit(solution)/shard_map/ppermute | solution.py:231
  251.4 6.0 %collective-permute-start.26 = (bf16[304,128]{1,0:T(8,128)(2,1)}, bf16[304,128]{1,0:T(8,128)(2,1)}, u32[]{:S(2)}, u32[]{:S(2)}) collective-permute-start(bf16[304,128]{1,0:T(8,128)(2,1)} %get-tuple-element.175.refs_0_), channel_id=1, source_target_pairs={{0,2},{1,3},{2,0},{3,1},{4,6},{5,7},{6,4},{7,5},{8,10},{9,11},{10,... | collective-permute-start | bytes 233480 | tf_op jit(solution)/shard_map/ppermute | solution.py:231
  253.1 4.3 %collective-permute-start.25 = (bf16[304,128]{1,0:T(8,128)(2,1)}, bf16[304,128]{1,0:T(8,128)(2,1)}, u32[]{:S(2)}, u32[]{:S(2)}) collective-permute-start(bf16[304,128]{1,0:T(8,128)(2,1)} %get-tuple-element.175.refs_0_), channel_id=1, source_target_pairs={{0,1},{1,0},{2,3},{3,2},{4,5},{5,4},{6,7},{7,6},{8,9},{9,8},{10,11... | collective-permute-start | bytes 233480 | tf_op jit(solution)/shard_map/ppermute | solution.py:231
  282.8 14.5 %all-to-all-start.12 = ((f32[32,8,128]{2,1,0:T(8,128)}), f32[32,8,128]{2,1,0:T(8,128)}, u32[]{:S(2)}, u32[]{:S(2)}) async-start(f32[32,8,128]{2,1,0:T(8,128)} %get-tuple-element.184), calls=%async_computation.12 | async-start | bytes 262144 | tf_op jit(solution)/shard_map/all_to_all | solution.py:243
  286.8 1.9 collective-permute-start.28
  287.0 5.7 %collective-permute-start.29 = (bf16[304,128]{1,0:T(8,128)(2,1)S(1)}, bf16[304,128]{1,0:T(8,128)(2,1)}, u32[]{:S(2)}, u32[]{:S(2)}) collective-permute-start(bf16[304,128]{1,0:T(8,128)(2,1)S(1)} %copy-done.17), channel_id=1, source_target_pairs={{0,2},{1,3},{2,0},{3,1},{4,6},{5,7},{6,4},{7,5},{8,10},{9,11},{10,... | collective-permute-start | bytes 233480 | tf_op jit(solution)/shard_map/ppermute | solution.py:231
  287.4 6.3 %collective-permute-start.30 = (bf16[304,128]{1,0:T(8,128)(2,1)S(1)}, bf16[304,128]{1,0:T(8,128)(2,1)}, u32[]{:S(2)}, u32[]{:S(2)}) collective-permute-start(bf16[304,128]{1,0:T(8,128)(2,1)S(1)} %copy-done.15), channel_id=1, source_target_pairs={{0,3},{1,2},{2,1},{3,0},{4,7},{5,6},{6,5},{7,4},{8,11},{9,10},{10,... | collective-permute-start | bytes 233480 | tf_op jit(solution)/shard_map/ppermute | solution.py:231
  304.3 16.3 %collective-permute-start.34 = (bf16[4,576,128]{2,1,0:T(8,128)(2,1)}, bf16[4,576,128]{2,1,0:T(8,128)(2,1)}, u32[]{:S(2)}, u32[]{:S(2)}) collective-permute-start(bf16[4,576,128]{2,1,0:T(8,128)(2,1)} %get-tuple-element.205), channel_id=1, source_target_pairs={{0,4},{4,0},{8,12},{12,8},{16,20},{20,16},{24,28},{28,24},{1,5},{5... | collective-permute-start | bytes 1769480 | tf_op jit(solution)/shard_map/ppermute | solution.py:1053
  305.8 18.1 %collective-permute-start.31 = (bf16[4,304,128]{2,1,0:T(8,128)(2,1)}, bf16[4,304,128]{2,1,0:T(8,128)(2,1)}, u32[]{:S(2)}, u32[]{:S(2)}) collective-permute-start(bf16[4,304,128]{2,1,0:T(8,128)(2,1)} %get-tuple-element.200), channel_id=1, source_target_pairs={{0,1},{1,0},{2,3},{3,2},{4,5},{5,4},{6,7},{7,6},{8,9},{9,8},{10,11... | collective-permute-start | bytes 933896 | tf_op jit(solution)/shard_map/ppermute | solution.py:231
  305.8 18.1 %collective-permute-start.32 = (bf16[4,304,128]{2,1,0:T(8,128)(2,1)}, bf16[4,304,128]{2,1,0:T(8,128)(2,1)}, u32[]{:S(2)}, u32[]{:S(2)}) collective-permute-start(bf16[4,304,128]{2,1,0:T(8,128)(2,1)} %get-tuple-element.201), channel_id=1, source_target_pairs={{0,2},{1,3},{2,0},{3,1},{4,6},{5,7},{6,4},{7,5},{8,10},{9,11},{10,... | collective-permute-start | bytes 933896 | tf_op jit(solution)/shard_map/ppermute | solution.py:231
  306.4 17.6 %collective-permute-start.33 = (bf16[4,304,128]{2,1,0:T(8,128)(2,1)}, bf16[4,304,128]{2,1,0:T(8,128)(2,1)}, u32[]{:S(2)}, u32[]{:S(2)}) collective-permute-start(bf16[4,304,128]{2,1,0:T(8,128)(2,1)} %get-tuple-element.202), channel_id=1, source_target_pairs={{0,3},{1,2},{2,1},{3,0},{4,7},{5,6},{6,5},{7,4},{8,11},{9,10},{10,... | collective-permute-start | bytes 933896 | tf_op jit(solution)/shard_map/ppermute | solution.py:231
  307.7 16.3 %all-to-all-start.13 = ((f32[32,8,128]{2,1,0:T(8,128)}), f32[32,8,128]{2,1,0:T(8,128)}, u32[]{:S(2)}, u32[]{:S(2)}) async-start(f32[32,8,128]{2,1,0:T(8,128)} %get-tuple-element.198), calls=%async_computation.14 | async-start | bytes 262144 | tf_op jit(solution)/shard_map/all_to_all | solution.py:243
  311.1 55.7 %reduce-scatter.8.cloned.1.call-start = ((), (), s32[]{:S(2)}) async-start(), calls=%async_computation.20 | async-start | bytes 737280 | tf_op jit(solution)/shard_map/reduce_scatter | solution.py:1074
  329.1 2.3 collective-permute-start.36
  329.3 33.6 %collective-permute-start.35 = (bf16[4,304,256]{2,1,0:T(8,128)(2,1)}, bf16[4,304,256]{2,1,0:T(8,128)(2,1)}, u32[]{:S(2)}, u32[]{:S(2)}) collective-permute-start(bf16[4,304,256]{2,1,0:T(8,128)(2,1)} %get-tuple-element.207), channel_id=1, source_target_pairs={{0,1},{1,0},{2,3},{3,2},{4,5},{5,4},{6,7},{7,6},{8,9},{9,8},{10,11... | collective-permute-start | bytes 1867784 | tf_op jit(solution)/shard_map/ppermute | solution.py:231
  333.4 29.5 %collective-permute-start.37 = (bf16[4,304,256]{2,1,0:T(8,128)(2,1)}, bf16[4,304,256]{2,1,0:T(8,128)(2,1)}, u32[]{:S(2)}, u32[]{:S(2)}) collective-permute-start(bf16[4,304,256]{2,1,0:T(8,128)(2,1)} %add_convert_fusion.refs_6_.refs_5_), channel_id=1, source_target_pairs={{0,2},{1,3},{2,0},{3,1},{4,6},{5,7},{6,4},{7,5},{8,10},{9,11},{10,... | collective-permute-start | bytes 1867784 | tf_op jit(solution)/shard_map/ppermute | solution.py:231
  335.7 18.2 %collective-permute-start.39 = (bf16[1024,128]{1,0:T(8,128)(2,1)}, bf16[1024,128]{1,0:T(8,128)(2,1)}, u32[]{:S(2)}, u32[]{:S(2)}) collective-permute-start(bf16[1024,128]{1,0:T(8,128)(2,1)} %dynamic-slice_bitcast_fusion), channel_id=1, source_target_pairs={{0,4},{4,0},{8,12},{12,8},{16,20},{20,16},{24,28},{28,24},{1,5},{5... | collective-permute-start | bytes 786440 | tf_op jit(solution)/shard_map/ppermute | solution.py:914
  339.9 31.4 %all-to-all-start.14 = ((bf16[8,128,128]{2,1,0:T(8,128)(2,1)}), bf16[8,128,128]{2,1,0:T(8,128)(2,1)}, u32[]{:S(2)}, u32[]{:S(2)}) async-start(bf16[8,128,128]{2,1,0:T(8,128)(2,1)} %shard_map.393), calls=%async_computation.17 | async-start | bytes 524288 | tf_op jit(solution)/shard_map/all_to_all | solution.py:240
  344.9 9.0 %collective-permute-start.38 = (bf16[832,128]{1,0:T(8,128)(2,1)S(1)}, bf16[832,128]{1,0:T(8,128)(2,1)}, u32[]{:S(2)}, u32[]{:S(2)}) collective-permute-start(bf16[832,128]{1,0:T(8,128)(2,1)S(1)} %dynamic-slice_bitcast_fusion.1), channel_id=1, source_target_pairs={{0,4},{4,0},{8,12},{12,8},{16,20},{20,16},{24,28},{28,24},{1,5},{5... | collective-permute-start | bytes 638984 | tf_op jit(solution)/shard_map/ppermute | solution.py:914
  356.2 15.1 %collective-permute-start.40 = (bf16[768,128]{1,0:T(8,128)(2,1)}, bf16[768,128]{1,0:T(8,128)(2,1)}, u32[]{:S(2)}, u32[]{:S(2)}) collective-permute-start(bf16[768,128]{1,0:T(8,128)(2,1)} %get-tuple-element.217), channel_id=1, source_target_pairs={{0,0},{1,8},{2,16},{3,24},{4,4},{5,12},{6,20},{7,28},{8,1},{9,9},{... | collective-permute-start | bytes 589832 | tf_op jit(solution)/shard_map/ppermute | solution.py:252
  (15 other events, 83.0 us)
Sparse Core Ops, SparseCore 0:
  11.5 26.9 all-gather.6
  42.5 60.5 all-gather.8
  105.8 49.5 all-gather.10
  227.9 39.4 reduce-scatter.3
  282.9 45.8 reduce-scatter.5
  331.0 23.1 reduce-scatter.7
where the time goes:
time: 388 us; the launch traced here: 380 us
  waiting for transfers between devices  110 us (28%)
  Pallas kernels  99.3 us (26%)
  starting transfers between devices  92.7 us (24%)
  blocking collectives  50.5 us (13%)
  between operations  14.8 us (4%)
  other arithmetic  9.74 us (3%)
    pallas_call x27, Pallas kernels, call(): pl.pallas_call(body, grid=(1,), out_shape=tuple(outs), in_specs=[SM] + [b...  99.3 us
    all_to_all x4, blocking collectives, to_batch(): return lax.all_to_all(x, 'batch', 0, 0, tiled=True)  50.5 us
    ppermute x36, waiting for transfers between devices, chan_swap(): return lax.ppermute(x, 'chan', [(i, i ^ r) for i in range(nc)])  36.2 us
    all_to_all x8, starting transfers between devices, to_all(): return lax.all_to_all(x, ALL, 0, 0, tiled=True)  33.1 us
    ppermute x2, waiting for transfers between devices, turn_share(): return lax.ppermute(x, ALL, turn)  22.6 us
    ppermute x36, starting transfers between devices, chan_swap(): return lax.ppermute(x, 'chan', [(i, i ^ r) for i in range(nc)])  21.4 us
    all_to_all x3, waiting for transfers between devices, to_batch(): return lax.all_to_all(x, 'batch', 0, 0, tiled=True)  16.7 us
    all_to_all x3, starting transfers between devices, to_batch(): return lax.all_to_all(x, 'batch', 0, 0, tiled=True)  14.4 us
  transfers between devices with their start and end apart: 58, of which 25 were waited for; matrix products, arithmetic and copies ran while one was open for 3% of the time, Pallas kernels for 18%

commit v1 on v0

--- a/solution.py
+++ b/solution.py
@@ -894,7 +894,9 @@
         gw2[...] = six[0:1, :]
         bw2[...] = six[1:2, :]
 
-    def own_kernel(p_ref, turned_ref, one_ref, reduce_ref, e1_out, r2_out, e2_out, s1_out, r1_out):
+    def own_kernel(p_ref, turned_ref, one_ref, reduce_ref, *rest):
+        params_in, (e1_out, r2_out, e2_out, s1_out, r1_out, *params_out) = rest[:6], rest[6:]
+        param_kernel(p_ref, *params_in, *params_out)
         s1_out[...] = one_ref[...].astype(F32)
         total = reduce_ref[0].astype(F32)
         for b in range(1, nb):
@@ -1075,7 +1077,8 @@
         sum_one, "batch", scatter_dimension=0, tiled=False,
         axis_index_groups=[list(range(first, nb, 2)) for first in range(2)],
     )
-    e1_own, r2_own, e2_own, s1_total, r1_out = call(
+    mid_pair, wide_pair, wide_row = struct((2, mid)), struct((2, wide)), struct((1, wide))
+    e1_own, r2_own, e2_own, s1_total, r1_out, *own_params_grad = call(
         own_kernel,
         (
             struct((mid, e_cols)),
@@ -1083,14 +1086,9 @@
             struct((mid, e_cols)),
             struct((9 * s_rows, mid)),
             struct((in_rows, mid)),
+            mid_pair, mid_pair, wide_pair, wide_pair, mid_pair, mid_pair, wide_row, wide_row,
         ),
-        place, turn_share(turned), s1_total, to_batch(shares),
-    )
-    mid_pair, wide_pair, wide_row = struct((2, mid)), struct((2, wide)), struct((1, wide))
-    own_params_grad = call(
-        param_kernel,
-        (mid_pair, mid_pair, wide_pair, wide_pair, mid_pair, mid_pair, wide_row, wide_row),
-        place, par_one, par_two, par_wide, par_four, par_five, par_six, after=[far_sum],
+        place, turn_share(turned), s1_total, to_batch(shares), par_one, par_two, par_wide, par_four, par_five, par_six,
     )
     outs = (
         output,
@@ -1106,7 +1104,6 @@
     )
     (input_grad,) = call(
         input_kernel, (struct((side, side, crops, part_in)),), place, slots[0], own_back, far_back, seg_full,
-        after=[own_params_grad[0]],
     )
     return outs[:1] + (input_grad.transpose(2, 0, 1, 3), r1_out) + outs[1:]
 

time: 388 us -> 388 us (level)
    pallas_call x27 -> x26, Pallas kernels: 99.3 us -> 98 us  [call(): pl.pallas_call(body, grid=(1,), out_shape=tuple(outs), in_specs=[SM] + [b...]
  transfers between devices with their start and end apart: 58 -> 58, of which waited for: 25 -> 25; matrix products, arithmetic and copies ran while one was open for 3% -> 3% of each run, Pallas kernels for 18% -> 17%
where the time goes in v1:
time: 388 us; the launch traced here: 380 us
  waiting for transfers between devices  111 us (29%)
  Pallas kernels  98 us (25%)
  starting transfers between devices  92.7 us (24%)
  blocking collectives  50.5 us (13%)
  between operations  14.8 us (4%)
  other arithmetic  9.7 us (2%)
    pallas_call x26, Pallas kernels, call(): pl.pallas_call(body, grid=(1,), out_shape=tuple(outs), in_specs=[SM] + [b...  98 us
    all_to_all x4, blocking collectives, to_batch(): return lax.all_to_all(x, 'batch', 0, 0, tiled=True)  50.5 us
    ppermute x36, waiting for transfers between devices, chan_swap(): return lax.ppermute(x, 'chan', [(i, i ^ r) for i in range(nc)])  36.2 us
    all_to_all x8, starting transfers between devices, to_all(): return lax.all_to_all(x, ALL, 0, 0, tiled=True)  33.1 us
    ppermute x2, waiting for transfers between devices, turn_share(): return lax.ppermute(x, ALL, turn)  24 us
    ppermute x36, starting transfers between devices, chan_swap(): return lax.ppermute(x, 'chan', [(i, i ^ r) for i in range(nc)])  21.4 us
    all_to_all x3, waiting for transfers between devices, to_batch(): return lax.all_to_all(x, 'batch', 0, 0, tiled=True)  16.8 us
    all_to_all x3, starting transfers between devices, to_batch(): return lax.all_to_all(x, 'batch', 0, 0, tiled=True)  14.4 us
  transfers between devices with their start and end apart: 58, of which 25 were waited for; matrix products, arithmetic and copies ran while one was open for 3% of the time, Pallas kernels for 17%

profile of v1, /device:TPU:4, one launch (start us, length us, event | category | flops | bytes accessed | tf_op | source)
XLA Modules:
  0.0 380.3 jit_solution(4781898773196002042)
XLA Ops:
  7.8 3.5 shard_map.368
  11.4 5.9 %all-to-all-start = ((bf16[8,256,128]{2,1,0:T(8,128)(2,1)}), bf16[8,256,128]{2,1,0:T(8,128)(2,1)}, u32[]{:S(2)}, u32[]{:S(2)}) async-start(bf16[8,256,128]{2,1,0:T(8,128)(2,1)} %get-tuple-element.126), calls=%async_computation | async-start | bytes 1048576 | tf_op jit(solution)/shard_map/all_to_all | solution.py:240
  17.4 4.7 %collective-permute-start.9 = (bf16[768,128]{1,0:T(8,128)(2,1)S(1)}, bf16[768,128]{1,0:T(8,128)(2,1)}, u32[]{:S(2)}, u32[]{:S(2)}) collective-permute-start(bf16[768,128]{1,0:T(8,128)(2,1)S(1)} %copy-done.12), channel_id=1, source_target_pairs={{0,0},{1,8},{2,16},{3,24},{4,4},{5,12},{6,20},{7,28},{8,1},{9,9},{... | collective-permute-start | bytes 589832 | tf_op jit(solution)/shard_map/ppermute | solution.py:252
  22.1 18.2 %collective-permute-done.9.refs_0_ = bf16[768,128]{1,0:T(8,128)(2,1)} collective-permute-done((bf16[768,128]{1,0:T(8,128)(2,1)S(1)}, bf16[768,128]{1,0:T(8,128)(2,1)}, u32[]{:S(2)}, u32[]{:S(2)}) %collective-permute-start.9) | collective-permute-done | bytes 196640 | tf_op jit(solution)/shard_map/ppermute | solution.py:252
  40.3 1.9 shard_map.372
  42.3 4.4 %all-to-all-start.1 = ((bf16[8,448,128]{2,1,0:T(8,128)(2,1)}), bf16[8,448,128]{2,1,0:T(8,128)(2,1)}, u32[]{:S(2)}, u32[]{:S(2)}) async-start(bf16[8,448,128]{2,1,0:T(8,128)(2,1)} %get-tuple-element.129), calls=%async_computation.1 | async-start | bytes 1835008 | tf_op jit(solution)/shard_map/all_to_all | solution.py:240
  52.5 3.8 shard_map.369
  56.3 2.0 collective-permute-start.2
  58.4 16.8 %all-to-all-done.1.refs_1_.refs_13_.refs_14_.refs_15_.refs_16_.refs_17_.refs_18_.refs_19_.refs_20_.refs_21_.refs_22_ = bf16[8,448,128]{2,1,0:T(8,128)(2,1)} async-done(((bf16[8,448,128]{2,1,0:T(8,128)(2,1)}), bf16[8,448,128]{2,1,0:T(8,128)(2,1)}, u32[]{:S(2)}, u32[]{:S(2)}) %all-to-all-start.1) | async-done | bytes 917536 | tf_op jit(solution)/shard_map/all_to_all | solution.py:240
  76.7 4.8 %all-to-all-start.2 = ((f32[32,8,128]{2,1,0:T(8,128)}), f32[32,8,128]{2,1,0:T(8,128)}, u32[]{:S(2)}, u32[]{:S(2)}) async-start(f32[32,8,128]{2,1,0:T(8,128)} %shard_map.370), calls=%async_computation.2 | async-start | bytes 262144 | tf_op jit(solution)/shard_map/all_to_all | solution.py:243
  83.0 2.8 collective-permute-done.5
  87.1 4.7 %all-to-all-done.2.refs_4_ = f32[32,8,128]{2,1,0:T(8,128)} async-done(((f32[32,8,128]{2,1,0:T(8,128)}), f32[32,8,128]{2,1,0:T(8,128)}, u32[]{:S(2)}, u32[]{:S(2)}) %all-to-all-start.2) | async-done | bytes 131104 | tf_op jit(solution)/shard_map/all_to_all | solution.py:243
  92.4 7.7 %shard_map.371 = (bf16[4,4,304,128]{3,2,1,0:T(8,128)(2,1)}, bf16[4,4,304,128]{3,2,1,0:T(8,128)(2,1)}, bf16[4,4,304,128]{3,2,1,0:T(8,128)(2,1)}, f32[8,128]{1,0:T...) custom-call(s32[2]{0:T(128)} %pad_add_fusion.p_ref, bf16[4,304,128]{2,1,0:T(8,128)(2,1)} %get-tuple-element.127.refs_0_, ...), custom_call_target="tpu_custom_call" | custom-call | flops 1593835520 | bytes 6609408 | tf_op jit(solution)/shard_map/pallas_call | solution.py:100
  100.1 3.9 %all-to-all-start.3 = ((f32[32,8,128]{2,1,0:T(8,128)}), f32[32,8,128]{2,1,0:T(8,128)}, u32[]{:S(2)}, u32[]{:S(2)}) async-start(f32[32,8,128]{2,1,0:T(8,128)} %get-tuple-element.131), calls=%async_computation.3 | async-start | bytes 262144 | tf_op jit(solution)/shard_map/all_to_all | solution.py:243
  106.0 2.9 shard_map.373.refs_10_.refs_2_
  109.5 2.2 collective-permute-done.7.refs_2_
  111.7 3.8 %shard_map.374 = (bf16[4,304,128]{2,1,0:T(8,128)(2,1)}, f32[4,304,128]{2,1,0:T(8,128)}, f32[4,304,128]{2,1,0:T(8,128)}, f32[8,128]{1,0:T(8,128)}, f32[304,512]{1,0:T(8,128)}, /*index=5*/f32[8,48,128]{2,1,0:T(8,128)}) custom-call(s32[2]{0:T(128)} %pad_add_fusion.p_ref, bf16[304,128]{1,0:T(8,128)(2,1)} %get-tuple-element.130.refs_0_, ...), custom_call_target="tpu_custom_call" | custom-call | flops 318767104 | bytes 4015616 | tf_op jit(solution)/shard_map/pallas_call | solution.py:100
  115.5 14.1 %all_to_all.75.refs_0_ = f32[8,48,128]{2,1,0:T(8,128)} all-to-all(f32[8,48,128]{2,1,0:T(8,128)} %get-tuple-element.136), channel_id=1, replica_groups=mesh['batch'=8,'chan'=4] {'batch'}, dimensions={0} | all-to-all | bytes 393216 | tf_op jit(solution)/shard_map/all_to_all | solution.py:240
  129.6 4.2 %shard_map.375 = (f32[304,512]{1,0:T(8,128)}, f32[304,512]{1,0:T(8,128)}, f32[304,512]{1,0:T(8,128)}, f32[304,512]{1,0:T(8,128)}, f32[8,512]{1,0:T(8,128)}, /*in...) custom-call(s32[2]{0:T(128)} %pad_add_fusion.p_ref, ...), custom_call_target="tpu_custom_call" | custom-call | flops 318767104 | bytes 5117440 | tf_op jit(solution)/shard_map/pallas_call | solution.py:100
  135.7 3.7 collective-permute-done.11.refs_2_
  140.1 2.0 shard_map.376
  142.0 4.1 %all-to-all-start.5 = ((f32[32,8,128]{2,1,0:T(8,128)}), f32[32,8,128]{2,1,0:T(8,128)}, u32[]{:S(2)}, u32[]{:S(2)}) async-start(f32[32,8,128]{2,1,0:T(8,128)} %get-tuple-element.143), calls=%async_computation.5 | async-start | bytes 262144 | tf_op jit(solution)/shard_map/all_to_all | solution.py:243
  148.1 7.4 %all-gather.11.cloned.1.call-done = bf16[6656,128]{1,0:T(8,128)(2,1)} async-done(((bf16[832,128]{1,0:T(8,128)(2,1)}), bf16[6656,128]{1,0:T(8,128)(2,1)}) %all-gather.11.cloned.1.call-update) | async-done | bytes 1703952 | tf_op jit(solution)/shard_map/all_gather | solution.py:282
  155.4 5.3 %shard_map.377 = (bf16[4,304,128]{2,1,0:T(8,128)(2,1)}, f32[4,304,128]{2,1,0:T(8,128)}, f32[4,304,128]{2,1,0:T(8,128)}, f32[8,128]{1,0:T(8,128)}, bf16[304,128]{1,0:T(8,128)(2,1)}, /*index=5*/f32[32,8,128]{2,1,0:T(8,128)}) custom-call(s32[2]{0:T(128)} %pad_add_fusion.p_ref, bf16[304,128]{1,0:T(8,128)(2,1)} %get-tuple-element.142.refs_0_, ...), custom_call_target="tpu_custom_call" | custom-call | flops 1275068416 | bytes 3457536 | tf_op jit(solution)/shard_map/pallas_call | solution.py:100
  160.7 3.7 all-to-all-start.6
  166.4 3.5 collective-permute-done.18.refs_3_
  169.9 2.2 collective-permute-done.17.refs_2_
  172.1 3.5 shard_map.378
  175.7 12.1 %all_to_all.76.refs_0_ = f32[8,24,128]{2,1,0:T(8,128)} all-to-all(f32[8,24,128]{2,1,0:T(8,128)} %get-tuple-element.147), channel_id=1, replica_groups=mesh['batch'=8,'chan'=4] {'batch'}, dimensions={0} | all-to-all | bytes 196608 | tf_op jit(solution)/shard_map/all_to_all | solution.py:240
  187.7 4.4 %shard_map.379 = (f32[7,7,16,512]{3,2,1,0:T(8,128)}, f32[304,512]{1,0:T(8,128)}, f32[304,512]{1,0:T(8,128)}, f32[8,512]{1,0:T(8,128)}, f32[8,24,128]{2,1,0:T(8,128)}) custom-call(s32[2]{0:T(128)} %pad_add_fusion.p_ref, f32[8,24,128]{2,1,0:T(8,128)} %all_to_all.76.refs_0_, f32[304,512]{1,0:T(8,128)} %get-tuple-element.148.refs_1_, ...), custom_call_target="tpu_custom_call" | custom-call | flops 100000000 | bytes 5137920 | tf_op jit(solution)/shard_map/pallas_call | solution.py:100
  192.2 11.1 %all_to_all.77.refs_0_ = f32[8,24,128]{2,1,0:T(8,128)} all-to-all(f32[8,24,128]{2,1,0:T(8,128)} %get-tuple-element.151), channel_id=1, replica_groups=mesh['batch'=8,'chan'=4] {'batch'}, dimensions={0} | all-to-all | bytes 196608 | tf_op jit(solution)/shard_map/all_to_all | solution.py:240
  203.3 3.6 shard_map.380
  206.8 3.9 %all-to-all-start.9 = ((f32[32,8,128]{2,1,0:T(8,128)}), f32[32,8,128]{2,1,0:T(8,128)}, u32[]{:S(2)}, u32[]{:S(2)}) async-start(f32[32,8,128]{2,1,0:T(8,128)} %get-tuple-element.157), calls=%async_computation.9 | async-start | bytes 262144 | tf_op jit(solution)/shard_map/all_to_all | solution.py:243
  212.7 4.4 %collective-permute-done.20.refs_3_ = bf16[304,128]{1,0:T(8,128)(2,1)} collective-permute-done((bf16[304,128]{1,0:T(8,128)(2,1)}, bf16[304,128]{1,0:T(8,128)(2,1)}, u32[]{:S(2)}, u32[]{:S(2)}) %collective-permute-start.20) | collective-permute-done | bytes 77856 | tf_op jit(solution)/shard_map/ppermute | solution.py:231
  218.0 5.7 %shard_map.381 = (bf16[304,1152]{1,0:T(8,128)(2,1)}, f32[8,128]{1,0:T(8,128)}, f32[32,8,128]{2,1,0:T(8,128)}, bf16[1,304,128]{2,1,0:T(8,128)(2,1)}, bf16[1,304,1...) custom-call(s32[2]{0:T(128)} %pad_add_fusion.p_ref, ...), custom_call_target="tpu_custom_call" | custom-call | flops 1275068416 | bytes 4233216 | tf_op jit(solution)/shard_map/pallas_call | solution.py:100
  223.7 3.9 %shard_map.382.refs_10_ = bf16[8,832,128]{2,1,0:T(8,128)(2,1)} custom-call(s32[2]{0:T(128)} %pad_add_fusion.p_ref, bf16[304,512]{1,0:T(8,128)(2,1)} %get-tuple-element.171.refs_0_, bf16[4,304,128]{2,1,0:T(8,128)(2,1)} %get-tuple-element.172.refs_1_, bf16[4,304,128]{2,1,0:T(8,128)(2,1)} %get-tuple-element.173.refs_2_, ...), custom_call_target="tpu_custom_call" | custom-call | flops 1593835520 | bytes 3338240 | tf_op jit(solution)/shard_map/pallas_call | solution.py:100
  227.7 5.3 %all-to-all-start.10 = ((f32[32,8,128]{2,1,0:T(8,128)}), f32[32,8,128]{2,1,0:T(8,128)}, u32[]{:S(2)}, u32[]{:S(2)}) async-start(f32[32,8,128]{2,1,0:T(8,128)} %get-tuple-element.165), calls=%async_computation.10 | async-start | bytes 262144 | tf_op jit(solution)/shard_map/all_to_all | solution.py:243
  233.0 9.5 %reduce-scatter.6.cloned.1.call-start = ((), (), s32[]{:S(2)}) async-start(), calls=%async_computation.19 | async-start | bytes 2621440 | tf_op jit(solution)/shard_map/reduce_scatter | solution.py:912
  244.5 3.6 collective-permute-done.23.refs_3_
  248.6 2.1 shard_map.383
  253.0 1.8 collective-permute-done.27.refs_3_
  254.8 2.5 collective-permute-done.26.refs_2_
  257.3 3.6 shard_map.384
  260.9 13.2 %all_to_all.78.refs_0_ = f32[8,40,128]{2,1,0:T(8,128)} all-to-all(f32[8,40,128]{2,1,0:T(8,128)} %get-tuple-element.179), channel_id=1, replica_groups=mesh['batch'=8,'chan'=4] {'batch'}, dimensions={0} | all-to-all | bytes 327680 | tf_op jit(solution)/shard_map/all_to_all | solution.py:240
  274.1 4.1 %shard_map.385 = (bf16[304,512]{1,0:T(8,128)(2,1)}, bf16[304,512]{1,0:T(8,128)(2,1)}, f32[8,512]{1,0:T(8,128)}, f32[32,8,128]{2,1,0:T(8,128)}, bf16[304,128]{1,0...) custom-call(s32[2]{0:T(128)} %pad_add_fusion.p_ref, ...), custom_call_target="tpu_custom_call" | custom-call | flops 318767104 | bytes 4916736 | tf_op jit(solution)/shard_map/pallas_call | solution.py:100
  278.2 4.5 %shard_map.386.refs_24_ = bf16[8,1024,128]{2,1,0:T(8,128)(2,1)} custom-call(s32[2]{0:T(128)} %pad_add_fusion.p_ref, bf16[304,512]{1,0:T(8,128)(2,1)} %get-tuple-element.193.refs_0_, bf16[4,304,128]{2,1,0:T(8,128)(2,1)} %get-tuple-element.194.refs_1_, bf16[304,512]{1,0:T(8,128)(2,1)} %get-tuple-element.195.refs_2_, ...), custom_call_target="tpu_custom_call" | custom-call | flops 1275068416 | bytes 4276224 | tf_op jit(solution)/shard_map/pallas_call | solution.py:100
  282.7 4.0 %all-to-all-start.12 = ((f32[32,8,128]{2,1,0:T(8,128)}), f32[32,8,128]{2,1,0:T(8,128)}, u32[]{:S(2)}, u32[]{:S(2)}) async-start(f32[32,8,128]{2,1,0:T(8,128)} %get-tuple-element.184), calls=%async_computation.12 | async-start | bytes 262144 | tf_op jit(solution)/shard_map/all_to_all | solution.py:243
  288.6 4.0 %collective-permute-done.29.refs_3_ = bf16[304,128]{1,0:T(8,128)(2,1)} collective-permute-done((bf16[304,128]{1,0:T(8,128)(2,1)S(1)}, bf16[304,128]{1,0:T(8,128)(2,1)}, u32[]{:S(2)}, u32[]{:S(2)}) %collective-permute-start.29) | collective-permute-done | bytes 77856 | tf_op jit(solution)/shard_map/ppermute | solution.py:231
  293.6 3.7 all-to-all-done.12.refs_0_
  297.3 7.0 %shard_map.387 = (bf16[4,576,128]{2,1,0:T(8,128)(2,1)}, bf16[4,576,128]{2,1,0:T(8,128)(2,1)}, f32[8,128]{1,0:T(8,128)}, f32[32,8,128]{2,1,0:T(8,128)}, bf16[4,30...) custom-call(s32[2]{0:T(128)} %pad_add_fusion.p_ref, ...), custom_call_target="tpu_custom_call" | custom-call | flops 2550136832 | bytes 8165888 | tf_op jit(solution)/shard_map/pallas_call | solution.py:100
  307.6 3.4 all-to-all-start.13
  311.1 9.4 %collective-permute-done.34.refs_1_ = bf16[4,576,128]{2,1,0:T(8,128)(2,1)} collective-permute-done((bf16[4,576,128]{2,1,0:T(8,128)(2,1)}, bf16[4,576,128]{2,1,0:T(8,128)(2,1)}, u32[]{:S(2)}, u32[]{:S(2)}) %collective-permute-start.34) | collective-permute-done | bytes 589856 | tf_op jit(solution)/shard_map/ppermute | solution.py:1055
  320.5 2.2 shard_map.388.refs_13_
  323.9 5.1 %shard_map.389 = (bf16[4,304,128]{2,1,0:T(8,128)(2,1)}, f32[8,128]{1,0:T(8,128)}, bf16[4,304,256]{2,1,0:T(8,128)(2,1)}, bf16[4,304,256]{2,1,0:T(8,128)(2,1)}, bf...) custom-call(s32[2]{0:T(128)} %pad_add_fusion.p_ref, f32[32,8,128]{2,1,0:T(8,128)} %all-to-all-done.13.refs_0_, ...), custom_call_target="tpu_custom_call" | custom-call | flops 1275068416 | bytes 6178816 | tf_op jit(solution)/shard_map/pallas_call | solution.py:100
  331.3 2.1 add_convert_fusion.refs_5_
  336.3 3.5 shard_map.392
  339.8 4.1 %all-to-all-start.14 = ((bf16[8,128,128]{2,1,0:T(8,128)(2,1)}), bf16[8,128,128]{2,1,0:T(8,128)(2,1)}, u32[]{:S(2)}, u32[]{:S(2)}) async-start(bf16[8,128,128]{2,1,0:T(8,128)(2,1)} %shard_map.392), calls=%async_computation.17 | async-start | bytes 524288 | tf_op jit(solution)/shard_map/all_to_all | solution.py:240
  344.8 2.0 collective-permute-start.38
  346.8 7.0 %collective-permute-done.38.refs_1_ = bf16[832,128]{1,0:T(8,128)(2,1)} collective-permute-done((bf16[832,128]{1,0:T(8,128)(2,1)S(1)}, bf16[832,128]{1,0:T(8,128)(2,1)}, u32[]{:S(2)}, u32[]{:S(2)}) %collective-permute-start.38) | collective-permute-done | bytes 213024 | tf_op jit(solution)/shard_map/ppermute | solution.py:916
  353.8 2.3 shard_map.391
  356.1 5.3 %collective-permute-start.40 = (bf16[768,128]{1,0:T(8,128)(2,1)}, bf16[768,128]{1,0:T(8,128)(2,1)}, u32[]{:S(2)}, u32[]{:S(2)}) collective-permute-start(bf16[768,128]{1,0:T(8,128)(2,1)} %get-tuple-element.210), channel_id=1, source_target_pairs={{0,0},{1,8},{2,16},{3,24},{4,4},{5,12},{6,20},{7,28},{8,1},{9,9},{... | collective-permute-start | bytes 589832 | tf_op jit(solution)/shard_map/ppermute | solution.py:252
  361.4 3.9 %shard_map.390 = f32[14,14,16,256]{3,2,1,0:T(8,128)} custom-call(s32[2]{0:T(128)} %pad_add_fusion.p_ref, bf16[4,304,256]{2,1,0:T(8,128)(2,1)} %get-tuple-element.206.refs_0_, bf16[4,304,256]{2,1,0:T(8,128)(2,1)} %collective-permute-done.35.refs_1_, bf16[4,304,256]{2,1,0:T(8,128)(2,1)} %collective-permute-done.37.refs_2_, ...), custom_call_target="tpu_custom_call" | custom-call | flops 100000000 | bytes 5117952 | tf_op jit(solution)/shard_map/pallas_call | solution.py:100
  365.3 5.9 %collective-permute-done.40.refs_0_ = bf16[768,128]{1,0:T(8,128)(2,1)} collective-permute-done((bf16[768,128]{1,0:T(8,128)(2,1)}, bf16[768,128]{1,0:T(8,128)(2,1)}, u32[]{:S(2)}, u32[]{:S(2)}) %collective-permute-start.40) | collective-permute-done | bytes 196640 | tf_op jit(solution)/shard_map/ppermute | solution.py:252
  371.2 2.1 shard_map.393
  (152 shorter events, 42.0 us)
Async XLA Ops:
  7.2 45.3 %all-gather.7.cloned.1.call-start = ((), (), s32[]{:S(2)}) async-start(), calls=%async_computation.21 | async-start | bytes 3112960 | tf_op jit(solution)/shard_map/all_gather | solution.py:300
  11.4 28.9 %all-to-all-start = ((bf16[8,256,128]{2,1,0:T(8,128)(2,1)}), bf16[8,256,128]{2,1,0:T(8,128)(2,1)}, u32[]{:S(2)}, u32[]{:S(2)}) async-start(bf16[8,256,128]{2,1,0:T(8,128)(2,1)} %get-tuple-element.126), calls=%async_computation | async-start | bytes 1048576 | tf_op jit(solution)/shard_map/all_to_all | solution.py:240
  17.3 88.7 %all-gather.9.cloned.1.call-start = ((), (), s32[]{:S(2)}) async-start(), calls=%async_computation.22 | async-start | bytes 2359296 | tf_op jit(solution)/shard_map/all_gather | solution.py:282
  17.4 22.9 %collective-permute-start.9 = (bf16[768,128]{1,0:T(8,128)(2,1)S(1)}, bf16[768,128]{1,0:T(8,128)(2,1)}, u32[]{:S(2)}, u32[]{:S(2)}) collective-permute-start(bf16[768,128]{1,0:T(8,128)(2,1)S(1)} %copy-done.12), channel_id=1, source_target_pairs={{0,0},{1,8},{2,16},{3,24},{4,4},{5,12},{6,20},{7,28},{8,1},{9,9},{... | collective-permute-start | bytes 589832 | tf_op jit(solution)/shard_map/ppermute | solution.py:252
  42.2 6.2 %copy-start.1 = (s32[304,1]{0,1:T(1,128)S(1)}, s32[304,1]{0,1:T(1,128)}, u32[]{:S(2)}) copy-start(s32[304,1]{0,1:T(1,128)} %constant.94) | copy-start | bytes 3652
  42.2 6.2 %copy-start.2 = (s32[304,1]{0,1:T(1,128)S(1)}, s32[304,1]{0,1:T(1,128)}, u32[]{:S(2)}) copy-start(s32[304,1]{0,1:T(1,128)} %constant.93) | copy-start | bytes 3652
  42.2 6.2 %copy-start.3 = (s32[304,1]{0,1:T(1,128)S(1)}, s32[304,1]{0,1:T(1,128)}, u32[]{:S(2)}) copy-start(s32[304,1]{0,1:T(1,128)} %constant.92) | copy-start | bytes 3652
  42.3 32.8 %all-to-all-start.1 = ((bf16[8,448,128]{2,1,0:T(8,128)(2,1)}), bf16[8,448,128]{2,1,0:T(8,128)(2,1)}, u32[]{:S(2)}, u32[]{:S(2)}) async-start(bf16[8,448,128]{2,1,0:T(8,128)(2,1)} %get-tuple-element.129), calls=%async_computation.1 | async-start | bytes 1835008 | tf_op jit(solution)/shard_map/all_to_all | solution.py:240
  46.7 108.7 %all-gather.11.cloned.1.call-start = ((), (), s32[]{:S(2)}) async-start(), calls=%async_computation.23 | async-start | bytes 1916928 | tf_op jit(solution)/shard_map/all_gather | solution.py:282
  48.1 34.3 %collective-permute-start.4 = (f32[8,128]{1,0:T(8,128)}, f32[8,128]{1,0:T(8,128)}, u32[]{:S(2)}, u32[]{:S(2)}) collective-permute-start(f32[8,128]{1,0:T(8,128)} %get-tuple-element.244), channel_id=1, source_target_pairs={{0,2},{1,3},{2,0},{3,1},{4,6},{5,7},{6,4},{7,5},{8,10},{9,11},{10,... | collective-permute-start | bytes 12296 | tf_op jit(solution)/shard_map/ppermute | solution.py:231
  48.1 34.9 %collective-permute-start.3 = (f32[8,128]{1,0:T(8,128)}, f32[8,128]{1,0:T(8,128)}, u32[]{:S(2)}, u32[]{:S(2)}) collective-permute-start(f32[8,128]{1,0:T(8,128)} %get-tuple-element.244), channel_id=1, source_target_pairs={{0,1},{1,0},{2,3},{3,2},{4,5},{5,4},{6,7},{7,6},{8,9},{9,8},{10,11... | collective-permute-start | bytes 12296 | tf_op jit(solution)/shard_map/ppermute | solution.py:231
  56.3 35.5 %collective-permute-start.2 = (bf16[4,304,128]{2,1,0:T(8,128)(2,1)}, bf16[4,304,128]{2,1,0:T(8,128)(2,1)}, u32[]{:S(2)}, u32[]{:S(2)}) collective-permute-start(bf16[4,304,128]{2,1,0:T(8,128)(2,1)} %get-tuple-element.127.refs_0_), channel_id=1, source_target_pairs={{0,3},{1,2},{2,1},{3,0},{4,7},{5,6},{6,5},{7,4},{8,11},{9,10},{10,... | collective-permute-start | bytes 933896 | tf_op jit(solution)/shard_map/ppermute | solution.py:231
  58.2 33.5 %collective-permute-start.1 = (bf16[4,304,128]{2,1,0:T(8,128)(2,1)}, bf16[4,304,128]{2,1,0:T(8,128)(2,1)}, u32[]{:S(2)}, u32[]{:S(2)}) collective-permute-start(bf16[4,304,128]{2,1,0:T(8,128)(2,1)} %get-tuple-element.127.refs_0_), channel_id=1, source_target_pairs={{0,2},{1,3},{2,0},{3,1},{4,6},{5,7},{6,4},{7,5},{8,10},{9,11},{10,... | collective-permute-start | bytes 933896 | tf_op jit(solution)/shard_map/ppermute | solution.py:231
  58.3 33.4 %collective-permute-start = (bf16[4,304,128]{2,1,0:T(8,128)(2,1)}, bf16[4,304,128]{2,1,0:T(8,128)(2,1)}, u32[]{:S(2)}, u32[]{:S(2)}) collective-permute-start(bf16[4,304,128]{2,1,0:T(8,128)(2,1)} %get-tuple-element.127.refs_0_), channel_id=1, source_target_pairs={{0,1},{1,0},{2,3},{3,2},{4,5},{5,4},{6,7},{7,6},{8,9},{9,8},{10,11... | collective-permute-start | bytes 933896 | tf_op jit(solution)/shard_map/ppermute | solution.py:231
  76.7 15.0 %all-to-all-start.2 = ((f32[32,8,128]{2,1,0:T(8,128)}), f32[32,8,128]{2,1,0:T(8,128)}, u32[]{:S(2)}, u32[]{:S(2)}) async-start(f32[32,8,128]{2,1,0:T(8,128)} %shard_map.370), calls=%async_computation.2 | async-start | bytes 262144 | tf_op jit(solution)/shard_map/all_to_all | solution.py:243
  82.4 3.3 collective-permute-start.5
  100.1 11.6 %all-to-all-start.3 = ((f32[32,8,128]{2,1,0:T(8,128)}), f32[32,8,128]{2,1,0:T(8,128)}, u32[]{:S(2)}, u32[]{:S(2)}) async-start(f32[32,8,128]{2,1,0:T(8,128)} %get-tuple-element.131), calls=%async_computation.3 | async-start | bytes 262144 | tf_op jit(solution)/shard_map/all_to_all | solution.py:243
  104.0 5.4 %collective-permute-start.8 = (bf16[304,128]{1,0:T(8,128)(2,1)}, bf16[304,128]{1,0:T(8,128)(2,1)}, u32[]{:S(2)}, u32[]{:S(2)}) collective-permute-start(bf16[304,128]{1,0:T(8,128)(2,1)} %get-tuple-element.130.refs_0_), channel_id=1, source_target_pairs={{0,3},{1,2},{2,1},{3,0},{4,7},{5,6},{6,5},{7,4},{8,11},{9,10},{10,... | collective-permute-start | bytes 233480 | tf_op jit(solution)/shard_map/ppermute | solution.py:231
  104.2 7.4 %collective-permute-start.7 = (bf16[304,128]{1,0:T(8,128)(2,1)}, bf16[304,128]{1,0:T(8,128)(2,1)}, u32[]{:S(2)}, u32[]{:S(2)}) collective-permute-start(bf16[304,128]{1,0:T(8,128)(2,1)} %get-tuple-element.130.refs_0_), channel_id=1, source_target_pairs={{0,2},{1,3},{2,0},{3,1},{4,6},{5,7},{6,4},{7,5},{8,10},{9,11},{10,... | collective-permute-start | bytes 233480 | tf_op jit(solution)/shard_map/ppermute | solution.py:231
  105.9 5.8 %collective-permute-start.6 = (bf16[304,128]{1,0:T(8,128)(2,1)}, bf16[304,128]{1,0:T(8,128)(2,1)}, u32[]{:S(2)}, u32[]{:S(2)}) collective-permute-start(bf16[304,128]{1,0:T(8,128)(2,1)} %get-tuple-element.130.refs_0_), channel_id=1, source_target_pairs={{0,1},{1,0},{2,3},{3,2},{4,5},{5,4},{6,7},{7,6},{8,9},{9,8},{10,11... | collective-permute-start | bytes 233480 | tf_op jit(solution)/shard_map/ppermute | solution.py:231
  133.8 1.9 collective-permute-start.10
  133.8 5.5 %collective-permute-start.11 = (bf16[304,128]{1,0:T(8,128)(2,1)}, bf16[304,128]{1,0:T(8,128)(2,1)}, u32[]{:S(2)}, u32[]{:S(2)}) collective-permute-start(bf16[304,128]{1,0:T(8,128)(2,1)} %get-tuple-element.140), channel_id=1, source_target_pairs={{0,2},{1,3},{2,0},{3,1},{4,6},{5,7},{6,4},{7,5},{8,10},{9,11},{10,... | collective-permute-start | bytes 233480 | tf_op jit(solution)/shard_map/ppermute | solution.py:231
  134.6 5.5 %collective-permute-start.12 = (bf16[304,128]{1,0:T(8,128)(2,1)}, bf16[304,128]{1,0:T(8,128)(2,1)}, u32[]{:S(2)}, u32[]{:S(2)}) collective-permute-start(bf16[304,128]{1,0:T(8,128)(2,1)} %get-tuple-element.141), channel_id=1, source_target_pairs={{0,3},{1,2},{2,1},{3,0},{4,7},{5,6},{6,5},{7,4},{8,11},{9,10},{10,... | collective-permute-start | bytes 233480 | tf_op jit(solution)/shard_map/ppermute | solution.py:231
  142.0 13.4 %all-to-all-start.5 = ((f32[32,8,128]{2,1,0:T(8,128)}), f32[32,8,128]{2,1,0:T(8,128)}, u32[]{:S(2)}, u32[]{:S(2)}) async-start(f32[32,8,128]{2,1,0:T(8,128)} %get-tuple-element.143), calls=%async_computation.5 | async-start | bytes 262144 | tf_op jit(solution)/shard_map/all_to_all | solution.py:243
  146.1 9.3 %collective-permute-start.15 = (bf16[304,128]{1,0:T(8,128)(2,1)}, bf16[304,128]{1,0:T(8,128)(2,1)}, u32[]{:S(2)}, u32[]{:S(2)}) collective-permute-start(bf16[304,128]{1,0:T(8,128)(2,1)} %get-tuple-element.142.refs_0_), channel_id=1, source_target_pairs={{0,3},{1,2},{2,1},{3,0},{4,7},{5,6},{6,5},{7,4},{8,11},{9,10},{10,... | collective-permute-start | bytes 233480 | tf_op jit(solution)/shard_map/ppermute | solution.py:231
  146.3 9.1 %collective-permute-start.14 = (bf16[304,128]{1,0:T(8,128)(2,1)}, bf16[304,128]{1,0:T(8,128)(2,1)}, u32[]{:S(2)}, u32[]{:S(2)}) collective-permute-start(bf16[304,128]{1,0:T(8,128)(2,1)} %get-tuple-element.142.refs_0_), channel_id=1, source_target_pairs={{0,2},{1,3},{2,0},{3,1},{4,6},{5,7},{6,4},{7,5},{8,10},{9,11},{10,... | collective-permute-start | bytes 233480 | tf_op jit(solution)/shard_map/ppermute | solution.py:231
  148.0 7.4 %collective-permute-start.13 = (bf16[304,128]{1,0:T(8,128)(2,1)}, bf16[304,128]{1,0:T(8,128)(2,1)}, u32[]{:S(2)}, u32[]{:S(2)}) collective-permute-start(bf16[304,128]{1,0:T(8,128)(2,1)} %get-tuple-element.142.refs_0_), channel_id=1, source_target_pairs={{0,1},{1,0},{2,3},{3,2},{4,5},{5,4},{6,7},{7,6},{8,9},{9,8},{10,11... | collective-permute-start | bytes 233480 | tf_op jit(solution)/shard_map/ppermute | solution.py:231
  160.7 11.4 %all-to-all-start.6 = ((f32[32,8,128]{2,1,0:T(8,128)}), f32[32,8,128]{2,1,0:T(8,128)}, u32[]{:S(2)}, u32[]{:S(2)}) async-start(f32[32,8,128]{2,1,0:T(8,128)} %get-tuple-element.146), calls=%async_computation.6 | async-start | bytes 262144 | tf_op jit(solution)/shard_map/all_to_all | solution.py:243
  164.5 5.4 %collective-permute-start.18 = (bf16[304,128]{1,0:T(8,128)(2,1)}, bf16[304,128]{1,0:T(8,128)(2,1)}, u32[]{:S(2)}, u32[]{:S(2)}) collective-permute-start(bf16[304,128]{1,0:T(8,128)(2,1)} %get-tuple-element.145.refs_0_), channel_id=1, source_target_pairs={{0,3},{1,2},{2,1},{3,0},{4,7},{5,6},{6,5},{7,4},{8,11},{9,10},{10,... | collective-permute-start | bytes 233480 | tf_op jit(solution)/shard_map/ppermute | solution.py:231
  164.7 7.4 %collective-permute-start.17 = (bf16[304,128]{1,0:T(8,128)(2,1)}, bf16[304,128]{1,0:T(8,128)(2,1)}, u32[]{:S(2)}, u32[]{:S(2)}) collective-permute-start(bf16[304,128]{1,0:T(8,128)(2,1)} %get-tuple-element.145.refs_0_), channel_id=1, source_target_pairs={{0,2},{1,3},{2,0},{3,1},{4,6},{5,7},{6,4},{7,5},{8,10},{9,11},{10,... | collective-permute-start | bytes 233480 | tf_op jit(solution)/shard_map/ppermute | solution.py:231
  166.3 5.8 %collective-permute-start.16 = (bf16[304,128]{1,0:T(8,128)(2,1)}, bf16[304,128]{1,0:T(8,128)(2,1)}, u32[]{:S(2)}, u32[]{:S(2)}) collective-permute-start(bf16[304,128]{1,0:T(8,128)(2,1)} %get-tuple-element.145.refs_0_), channel_id=1, source_target_pairs={{0,1},{1,0},{2,3},{3,2},{4,5},{5,4},{6,7},{7,6},{8,9},{9,8},{10,11... | collective-permute-start | bytes 233480 | tf_op jit(solution)/shard_map/ppermute | solution.py:231
  206.8 11.2 %all-to-all-start.9 = ((f32[32,8,128]{2,1,0:T(8,128)}), f32[32,8,128]{2,1,0:T(8,128)}, u32[]{:S(2)}, u32[]{:S(2)}) async-start(f32[32,8,128]{2,1,0:T(8,128)} %get-tuple-element.157), calls=%async_computation.9 | async-start | bytes 262144 | tf_op jit(solution)/shard_map/all_to_all | solution.py:243
  210.7 86.6 %reduce-scatter.4.cloned.1.call-start = ((), (), s32[]{:S(2)}) async-start(), calls=%async_computation.18 | async-start | bytes 2129920 | tf_op jit(solution)/shard_map/reduce_scatter | solution.py:912
  210.7 1.9 collective-permute-start.19
  210.9 6.1 %collective-permute-start.20 = (bf16[304,128]{1,0:T(8,128)(2,1)}, bf16[304,128]{1,0:T(8,128)(2,1)}, u32[]{:S(2)}, u32[]{:S(2)}) collective-permute-start(bf16[304,128]{1,0:T(8,128)(2,1)} %get-tuple-element.160), channel_id=1, source_target_pairs={{0,2},{1,3},{2,0},{3,1},{4,6},{5,7},{6,4},{7,5},{8,10},{9,11},{10,... | collective-permute-start | bytes 233480 | tf_op jit(solution)/shard_map/ppermute | solution.py:231
  211.3 6.7 %collective-permute-start.21 = (bf16[304,128]{1,0:T(8,128)(2,1)}, bf16[304,128]{1,0:T(8,128)(2,1)}, u32[]{:S(2)}, u32[]{:S(2)}) collective-permute-start(bf16[304,128]{1,0:T(8,128)(2,1)} %get-tuple-element.161), channel_id=1, source_target_pairs={{0,3},{1,2},{2,1},{3,0},{4,7},{5,6},{6,5},{7,4},{8,11},{9,10},{10,... | collective-permute-start | bytes 233480 | tf_op jit(solution)/shard_map/ppermute | solution.py:231
  227.6 14.9 %copy-start.16 = (bf16[1,304,128]{2,1,0:T(8,128)(2,1)S(1)}, bf16[1,304,128]{2,1,0:T(8,128)(2,1)}, u32[]{:S(2)}) copy-start(bf16[1,304,128]{2,1,0:T(8,128)(2,1)} %get-tuple-element.167) | copy-start | bytes 233476
  227.6 15.1 %copy-start.14 = (bf16[1,304,128]{2,1,0:T(8,128)(2,1)S(1)}, bf16[1,304,128]{2,1,0:T(8,128)(2,1)}, u32[]{:S(2)}) copy-start(bf16[1,304,128]{2,1,0:T(8,128)(2,1)} %get-tuple-element.168) | copy-start | bytes 233476
  227.7 15.5 %copy-start.13 = (bf16[1,304,128]{2,1,0:T(8,128)(2,1)S(1)}, bf16[1,304,128]{2,1,0:T(8,128)(2,1)}, u32[]{:S(2)}) copy-start(bf16[1,304,128]{2,1,0:T(8,128)(2,1)} %get-tuple-element.169) | copy-start | bytes 233476
  227.7 20.9 %all-to-all-start.10 = ((f32[32,8,128]{2,1,0:T(8,128)}), f32[32,8,128]{2,1,0:T(8,128)}, u32[]{:S(2)}, u32[]{:S(2)}) async-start(f32[32,8,128]{2,1,0:T(8,128)} %get-tuple-element.165), calls=%async_computation.10 | async-start | bytes 262144 | tf_op jit(solution)/shard_map/all_to_all | solution.py:243
  233.0 100.9 %reduce-scatter.6.cloned.1.call-start = ((), (), s32[]{:S(2)}) async-start(), calls=%async_computation.19 | async-start | bytes 2621440 | tf_op jit(solution)/shard_map/reduce_scatter | solution.py:912
  242.5 1.9 collective-permute-start.22
  242.7 5.3 %collective-permute-start.23 = (bf16[304,128]{1,0:T(8,128)(2,1)S(1)}, bf16[304,128]{1,0:T(8,128)(2,1)}, u32[]{:S(2)}, u32[]{:S(2)}) collective-permute-start(bf16[304,128]{1,0:T(8,128)(2,1)S(1)} %bitcast.106), channel_id=1, source_target_pairs={{0,2},{1,3},{2,0},{3,1},{4,6},{5,7},{6,4},{7,5},{8,10},{9,11},{10,... | collective-permute-start | bytes 233480 | tf_op jit(solution)/shard_map/ppermute | solution.py:231
  243.1 5.5 %collective-permute-start.24 = (bf16[304,128]{1,0:T(8,128)(2,1)S(1)}, bf16[304,128]{1,0:T(8,128)(2,1)}, u32[]{:S(2)}, u32[]{:S(2)}) collective-permute-start(bf16[304,128]{1,0:T(8,128)(2,1)S(1)} %bitcast.105), channel_id=1, source_target_pairs={{0,3},{1,2},{2,1},{3,0},{4,7},{5,6},{6,5},{7,4},{8,11},{9,10},{10,... | collective-permute-start | bytes 233480 | tf_op jit(solution)/shard_map/ppermute | solution.py:231
  250.7 4.1 %collective-permute-start.27 = (bf16[304,128]{1,0:T(8,128)(2,1)}, bf16[304,128]{1,0:T(8,128)(2,1)}, u32[]{:S(2)}, u32[]{:S(2)}) collective-permute-start(bf16[304,128]{1,0:T(8,128)(2,1)} %get-tuple-element.175.refs_0_), channel_id=1, source_target_pairs={{0,3},{1,2},{2,1},{3,0},{4,7},{5,6},{6,5},{7,4},{8,11},{9,10},{10,... | collective-permute-start | bytes 233480 | tf_op jit(solution)/shard_map/ppermute | solution.py:231
  251.4 6.0 %collective-permute-start.26 = (bf16[304,128]{1,0:T(8,128)(2,1)}, bf16[304,128]{1,0:T(8,128)(2,1)}, u32[]{:S(2)}, u32[]{:S(2)}) collective-permute-start(bf16[304,128]{1,0:T(8,128)(2,1)} %get-tuple-element.175.refs_0_), channel_id=1, source_target_pairs={{0,2},{1,3},{2,0},{3,1},{4,6},{5,7},{6,4},{7,5},{8,10},{9,11},{10,... | collective-permute-start | bytes 233480 | tf_op jit(solution)/shard_map/ppermute | solution.py:231
  253.0 4.3 %collective-permute-start.25 = (bf16[304,128]{1,0:T(8,128)(2,1)}, bf16[304,128]{1,0:T(8,128)(2,1)}, u32[]{:S(2)}, u32[]{:S(2)}) collective-permute-start(bf16[304,128]{1,0:T(8,128)(2,1)} %get-tuple-element.175.refs_0_), channel_id=1, source_target_pairs={{0,1},{1,0},{2,3},{3,2},{4,5},{5,4},{6,7},{7,6},{8,9},{9,8},{10,11... | collective-permute-start | bytes 233480 | tf_op jit(solution)/shard_map/ppermute | solution.py:231
  282.7 14.5 %all-to-all-start.12 = ((f32[32,8,128]{2,1,0:T(8,128)}), f32[32,8,128]{2,1,0:T(8,128)}, u32[]{:S(2)}, u32[]{:S(2)}) async-start(f32[32,8,128]{2,1,0:T(8,128)} %get-tuple-element.184), calls=%async_computation.12 | async-start | bytes 262144 | tf_op jit(solution)/shard_map/all_to_all | solution.py:243
  286.7 1.9 collective-permute-start.28
  286.9 5.7 %collective-permute-start.29 = (bf16[304,128]{1,0:T(8,128)(2,1)S(1)}, bf16[304,128]{1,0:T(8,128)(2,1)}, u32[]{:S(2)}, u32[]{:S(2)}) collective-permute-start(bf16[304,128]{1,0:T(8,128)(2,1)S(1)} %copy-done.17), channel_id=1, source_target_pairs={{0,2},{1,3},{2,0},{3,1},{4,6},{5,7},{6,4},{7,5},{8,10},{9,11},{10,... | collective-permute-start | bytes 233480 | tf_op jit(solution)/shard_map/ppermute | solution.py:231
  287.3 6.3 %collective-permute-start.30 = (bf16[304,128]{1,0:T(8,128)(2,1)S(1)}, bf16[304,128]{1,0:T(8,128)(2,1)}, u32[]{:S(2)}, u32[]{:S(2)}) collective-permute-start(bf16[304,128]{1,0:T(8,128)(2,1)S(1)} %copy-done.15), channel_id=1, source_target_pairs={{0,3},{1,2},{2,1},{3,0},{4,7},{5,6},{6,5},{7,4},{8,11},{9,10},{10,... | collective-permute-start | bytes 233480 | tf_op jit(solution)/shard_map/ppermute | solution.py:231
  304.2 16.3 %collective-permute-start.34 = (bf16[4,576,128]{2,1,0:T(8,128)(2,1)}, bf16[4,576,128]{2,1,0:T(8,128)(2,1)}, u32[]{:S(2)}, u32[]{:S(2)}) collective-permute-start(bf16[4,576,128]{2,1,0:T(8,128)(2,1)} %get-tuple-element.205), channel_id=1, source_target_pairs={{0,4},{4,0},{8,12},{12,8},{16,20},{20,16},{24,28},{28,24},{1,5},{5... | collective-permute-start | bytes 1769480 | tf_op jit(solution)/shard_map/ppermute | solution.py:1055
  305.8 18.1 %collective-permute-start.31 = (bf16[4,304,128]{2,1,0:T(8,128)(2,1)}, bf16[4,304,128]{2,1,0:T(8,128)(2,1)}, u32[]{:S(2)}, u32[]{:S(2)}) collective-permute-start(bf16[4,304,128]{2,1,0:T(8,128)(2,1)} %get-tuple-element.200), channel_id=1, source_target_pairs={{0,1},{1,0},{2,3},{3,2},{4,5},{5,4},{6,7},{7,6},{8,9},{9,8},{10,11... | collective-permute-start | bytes 933896 | tf_op jit(solution)/shard_map/ppermute | solution.py:231
  305.8 18.1 %collective-permute-start.32 = (bf16[4,304,128]{2,1,0:T(8,128)(2,1)}, bf16[4,304,128]{2,1,0:T(8,128)(2,1)}, u32[]{:S(2)}, u32[]{:S(2)}) collective-permute-start(bf16[4,304,128]{2,1,0:T(8,128)(2,1)} %get-tuple-element.201), channel_id=1, source_target_pairs={{0,2},{1,3},{2,0},{3,1},{4,6},{5,7},{6,4},{7,5},{8,10},{9,11},{10,... | collective-permute-start | bytes 933896 | tf_op jit(solution)/shard_map/ppermute | solution.py:231
  306.3 17.6 %collective-permute-start.33 = (bf16[4,304,128]{2,1,0:T(8,128)(2,1)}, bf16[4,304,128]{2,1,0:T(8,128)(2,1)}, u32[]{:S(2)}, u32[]{:S(2)}) collective-permute-start(bf16[4,304,128]{2,1,0:T(8,128)(2,1)} %get-tuple-element.202), channel_id=1, source_target_pairs={{0,3},{1,2},{2,1},{3,0},{4,7},{5,6},{6,5},{7,4},{8,11},{9,10},{10,... | collective-permute-start | bytes 933896 | tf_op jit(solution)/shard_map/ppermute | solution.py:231
  307.6 16.3 %all-to-all-start.13 = ((f32[32,8,128]{2,1,0:T(8,128)}), f32[32,8,128]{2,1,0:T(8,128)}, u32[]{:S(2)}, u32[]{:S(2)}) async-start(f32[32,8,128]{2,1,0:T(8,128)} %get-tuple-element.198), calls=%async_computation.14 | async-start | bytes 262144 | tf_op jit(solution)/shard_map/all_to_all | solution.py:243
  311.0 54.3 %reduce-scatter.8.cloned.1.call-start = ((), (), s32[]{:S(2)}) async-start(), calls=%async_computation.20 | async-start | bytes 737280 | tf_op jit(solution)/shard_map/reduce_scatter | solution.py:1076
  329.0 2.3 collective-permute-start.36
  329.3 32.2 %collective-permute-start.35 = (bf16[4,304,256]{2,1,0:T(8,128)(2,1)}, bf16[4,304,256]{2,1,0:T(8,128)(2,1)}, u32[]{:S(2)}, u32[]{:S(2)}) collective-permute-start(bf16[4,304,256]{2,1,0:T(8,128)(2,1)} %get-tuple-element.207), channel_id=1, source_target_pairs={{0,1},{1,0},{2,3},{3,2},{4,5},{5,4},{6,7},{7,6},{8,9},{9,8},{10,11... | collective-permute-start | bytes 1867784 | tf_op jit(solution)/shard_map/ppermute | solution.py:231
  333.4 28.1 %collective-permute-start.37 = (bf16[4,304,256]{2,1,0:T(8,128)(2,1)}, bf16[4,304,256]{2,1,0:T(8,128)(2,1)}, u32[]{:S(2)}, u32[]{:S(2)}) collective-permute-start(bf16[4,304,256]{2,1,0:T(8,128)(2,1)} %add_convert_fusion.refs_5_), channel_id=1, source_target_pairs={{0,2},{1,3},{2,0},{3,1},{4,6},{5,7},{6,4},{7,5},{8,10},{9,11},{10,... | collective-permute-start | bytes 1867784 | tf_op jit(solution)/shard_map/ppermute | solution.py:231
  335.6 18.2 %collective-permute-start.39 = (bf16[1024,128]{1,0:T(8,128)(2,1)}, bf16[1024,128]{1,0:T(8,128)(2,1)}, u32[]{:S(2)}, u32[]{:S(2)}) collective-permute-start(bf16[1024,128]{1,0:T(8,128)(2,1)} %dynamic-slice_bitcast_fusion), channel_id=1, source_target_pairs={{0,4},{4,0},{8,12},{12,8},{16,20},{20,16},{24,28},{28,24},{1,5},{5... | collective-permute-start | bytes 786440 | tf_op jit(solution)/shard_map/ppermute | solution.py:916
  339.8 31.4 %all-to-all-start.14 = ((bf16[8,128,128]{2,1,0:T(8,128)(2,1)}), bf16[8,128,128]{2,1,0:T(8,128)(2,1)}, u32[]{:S(2)}, u32[]{:S(2)}) async-start(bf16[8,128,128]{2,1,0:T(8,128)(2,1)} %shard_map.392), calls=%async_computation.17 | async-start | bytes 524288 | tf_op jit(solution)/shard_map/all_to_all | solution.py:240
  344.8 9.0 %collective-permute-start.38 = (bf16[832,128]{1,0:T(8,128)(2,1)S(1)}, bf16[832,128]{1,0:T(8,128)(2,1)}, u32[]{:S(2)}, u32[]{:S(2)}) collective-permute-start(bf16[832,128]{1,0:T(8,128)(2,1)S(1)} %dynamic-slice_bitcast_fusion.1), channel_id=1, source_target_pairs={{0,4},{4,0},{8,12},{12,8},{16,20},{20,16},{24,28},{28,24},{1,5},{5... | collective-permute-start | bytes 638984 | tf_op jit(solution)/shard_map/ppermute | solution.py:916
  356.1 15.1 %collective-permute-start.40 = (bf16[768,128]{1,0:T(8,128)(2,1)}, bf16[768,128]{1,0:T(8,128)(2,1)}, u32[]{:S(2)}, u32[]{:S(2)}) collective-permute-start(bf16[768,128]{1,0:T(8,128)(2,1)} %get-tuple-element.210), channel_id=1, source_target_pairs={{0,0},{1,8},{2,16},{3,24},{4,4},{5,12},{6,20},{7,28},{8,1},{9,9},{... | collective-permute-start | bytes 589832 | tf_op jit(solution)/shard_map/ppermute | solution.py:252
  (15 other events, 82.9 us)
Sparse Core Ops, SparseCore 0:
  11.5 26.9 all-gather.6
  42.4 60.5 all-gather.8
  105.8 49.5 all-gather.10
  227.8 39.4 reduce-scatter.3
  282.8 45.8 reduce-scatter.5
  330.9 23.1 reduce-scatter.7
